TPU v7x, 32 devices: a whole 2x2x4 slice. The times are simulated.
32 devices in a mesh: img: 2 (over y), gx: 4 (over z), gy: 4 (over x, core).
Axes of the slice: x: 2, y: 2, z: 4, core: 2. Of those that a mesh axis runs over, the one named last changes fastest.
Arguments:
- conc_old: float32 [128, 64, 128], P(('img', 'gx'), 'gy'), parts along dimension 0, may hold values from -1 to 1
- chem_old: float32 [128, 64, 128], P(('img', 'gx'), 'gy'), parts along dimension 0, may hold values from -4 to 4
Outputs:
- conc_new: float32 [128, 64, 128], P(('img', 'gx'), 'gy'), parts along dimension 0
- chem_new: float32 [128, 64, 128], P(('img', 'gx'), 'gy'), parts along dimension 0
There are 2 independent parts, one for each index of `img`. A program takes and returns all parts, laid end to end along the dimension named above; each array names one. Nothing has to cross between parts.
All inputs are finite; a program needn't handle non-finite values.
Results may differ from a plain program's by a relative error of at most 0.0001.
Values sent between devices are 32-bit elements; how exact they have to be, the bound alone decides.
A program may use at most 128 MiB of HBM per device.

v0:
```python
import jax
import jax.numpy as jnp
from jax import lax
from jax.sharding import PartitionSpec as P

LEVELS = 4
SWEEPS = 2
COARSE = 6


TIME_STEP = 32.0
GRADIENT_ENERGY = 0.5
STABILIZER = 2.0
DAMPING = 0.7


def extended(cells, sides, width):
    for axis, dim in sides:
        count = lax.axis_size(axis)
        head = lax.slice_in_dim(cells, 0, width, axis=dim)
        tail = lax.slice_in_dim(cells, cells.shape[dim] - width, cells.shape[dim], axis=dim)
        cells = jnp.concatenate(
            [
                lax.ppermute(tail, axis, [(i, (i + 1) % count) for i in range(count)]),
                cells,
                lax.ppermute(head, axis, [((i + 1) % count, i) for i in range(count)]),
            ],
            axis=dim,
        )
    return cells


def mobility_of(concentration):
    return 0.1 + jnp.square(1.0 - concentration * concentration)


def right_of(concentration):
    return jnp.stack(
        [
            concentration,
            concentration * concentration * concentration - (1.0 + STABILIZER) * concentration,
        ]
    )


def face_weights(mob_padded, level_scale):
    middle = mob_padded[1:-1, 1:-1, :]
    half_scale = 0.5 * level_scale
    weights = (
        half_scale * (middle + mob_padded[2:, 1:-1, :]),
        half_scale * (middle + mob_padded[:-2, 1:-1, :]),
        half_scale * (middle + mob_padded[1:-1, 2:, :]),
        half_scale * (middle + mob_padded[1:-1, :-2, :]),
        half_scale * (middle + jnp.roll(middle, -1, axis=2)),
        half_scale * (middle + jnp.roll(middle, 1, axis=2)),
    )
    total_weight = weights[0] + weights[1] + weights[2] + weights[3] + weights[4] + weights[5]
    return (weights, total_weight)


def neighbour_list(padded, middle):
    return (
        padded[2:, 1:-1, :],
        padded[:-2, 1:-1, :],
        padded[1:-1, 2:, :],
        padded[1:-1, :-2, :],
        jnp.roll(middle, -1, axis=2),
        jnp.roll(middle, 1, axis=2),
    )


def apply_operator(padded, weights, level_scale):
    middle = padded[:, 1:-1, 1:-1, :]
    conc_near = neighbour_list(padded[0], middle[0])
    chem_near = neighbour_list(padded[1], middle[1])
    flux = weights[0] * (chem_near[0] - middle[1])
    for position in range(1, 6):
        flux = flux + weights[position] * (chem_near[position] - middle[1])
    laplace = (
        conc_near[0]
        + conc_near[1]
        + conc_near[2]
        + conc_near[3]
        + conc_near[4]
        + conc_near[5]
        - 6.0 * middle[0]
    )
    first_eq = middle[0] - TIME_STEP * flux
    second_eq = middle[1] - STABILIZER * middle[0] + GRADIENT_ENERGY * level_scale * laplace
    return jnp.stack([first_eq, second_eq])


def update(residual, total_weight, level_scale):
    diagonal = STABILIZER + 6.0 * GRADIENT_ENERGY * level_scale
    coupling = TIME_STEP * total_weight
    determinant = 1.0 + coupling * diagonal
    conc_step = (residual[0] - coupling * residual[1]) / determinant
    chem_step = (residual[1] + diagonal * residual[0]) / determinant
    return DAMPING * jnp.stack([conc_step, chem_step])


def sweep_once(padded, right_side, mob_padded, level_scale):
    weights, total_weight = face_weights(mob_padded, level_scale)
    residual = right_side - apply_operator(padded, weights, level_scale)
    return padded[:, 1:-1, 1:-1, :] + update(residual, total_weight, level_scale)


def defect(padded, right_side, mob_padded, level_scale):
    weights = face_weights(mob_padded, level_scale)[0]
    return right_side - apply_operator(padded, weights, level_scale)


def coarsen(values):
    dims_now = values.shape
    grouped = values.reshape(
        dims_now[:-3] + (dims_now[-3] // 2, 2, dims_now[-2] // 2, 2, dims_now[-1] // 2, 2)
    )
    return jnp.sum(grouped, axis=(-5, -3, -1)) * 0.125


def refine(values):
    for axis_pos in (-3, -2, -1):
        values = jnp.repeat(values, 2, axis=axis_pos)
    return values


def trim_rim(values, width):
    return values[..., width:-width, width:-width, :]


def field_rim(fields):
    return extended(fields, (("gx", 1), ("gy", 2)), 1)


def coarsest_solve(right_side, mobility, level_scale):
    mob_padded = extended(mobility, (("gx", 0), ("gy", 1)), 1)
    fields = update(right_side, face_weights(mob_padded, level_scale)[1], level_scale)
    for sweep_index in range(COARSE - 1):
        padded = extended(fields, (("gx", 1), ("gy", 2)), 1)
        fields = sweep_once(padded, right_side, mob_padded, level_scale)
    return fields


def plain_solve(start_fields):
    outer_fields = field_rim(start_fields)
    mob_outer = mobility_of(outer_fields[0])
    mobility = trim_rim(mob_outer, 1)
    level_data = []
    for level_index in range(LEVELS - 1):
        if level_index == 0:
            mob_padded = mob_outer
        else:
            mob_padded = extended(mobility, (("gx", 0), ("gy", 1)), 1)
        level_data.append((mob_padded, 0.25**level_index))
        mobility = coarsen(mobility)
    coarsest_scale = 0.25 ** (LEVELS - 1)

    def cycle_level(level_index, right_side):
        if level_index == LEVELS - 1:
            return coarsest_solve(right_side, mobility, coarsest_scale)
        mob_padded, level_scale = level_data[level_index]
        if level_index == 0:
            fields = sweep_once(outer_fields, right_side, mob_padded, level_scale)
        else:
            fields = update(right_side, face_weights(mob_padded, level_scale)[1], level_scale)
        fields = sweep_once(field_rim(fields), right_side, mob_padded, level_scale)
        residual = defect(field_rim(fields), right_side, mob_padded, level_scale)
        fields = fields + refine(cycle_level(level_index + 1, coarsen(residual)))
        for sweep_index in range(SWEEPS):
            fields = sweep_once(field_rim(fields), right_side, mob_padded, level_scale)
        return fields

    return cycle_level(0, right_of(start_fields[0]))


def body(conc_old, chem_old):
    start_fields = jnp.stack([conc_old, chem_old])
    result = plain_solve(start_fields)
    return (result[0], result[1])


def solution(mesh):
    in_specs = (P(("img", "gx"), "gy", None), P(("img", "gx"), "gy", None))
    out_specs = (P(("img", "gx"), "gy", None), P(("img", "gx"), "gy", None))
    return jax.shard_map(body, mesh=mesh, in_specs=in_specs, out_specs=out_specs, check_vma=False)
```

profile of v0, /device:TPU:0, one launch (start us, length us, event | category | flops | bytes accessed | tf_op | source)
XLA Modules:
  0.0 302.8 jit_solution(2621444720984587918)
XLA Ops:
  1.4 3.0 collective-permute-start
  4.5 2.1 collective-permute-start.1
  10.8 1.8 collective-permute-start.3
  12.7 9.8 %stack.362 = f32[1,8,2,8,2,64,2]{6,5,4,3,2,1,0:T(8,128)} reshape(f32[16,16,128]{2,1,0:T(8,128)S(1)} %copy-done) | data formatting | bytes 262144 | tf_op jit(solution)/shard_map/stack | solution.py:38
  22.5 6.1 %copy.413 = f32[1,8,2,8,2,64,2]{5,3,6,4,2,1,0:T(8,128)} copy(f32[1,8,2,8,2,64,2]{6,5,4,3,2,1,0:T(8,128)} %stack.362) | data formatting | bytes 262144 | tf_op jit(solution)/shard_map/stack | solution.py:38
  31.5 9.8 %reshape.67 = f32[8,2,8,2,64,2]{5,4,3,2,1,0:T(8,128)} reshape(f32[16,16,128]{2,1,0:T(8,128)S(1)} %slice.2437) | data formatting | bytes 262144 | tf_op jit(solution)/shard_map/reshape | solution.py:115
  41.3 4.0 %reduce_sum.55 = f32[8,8,64]{2,1,0:T(8,128)S(1)} reduce(f32[8,2,8,2,64,2]{5,4,3,2,1,0:T(8,128)} %reshape.67, f32[]{:T(128)} %constant.30.clone.1), dimensions={1,3,5}, to_apply=%region_1.0 | reduce | flops 28672 | bytes 147460 | tf_op jit(solution)/shard_map/reduce_sum | solution.py:118
  51.0 3.8 %collective-permute-start.5 = (f32[2,1,16,128]{3,2,1,0:T(8,128)S(1)}, f32[2,1,16,128]{3,2,1,0:T(8,128)S(1)}, u32[]{:S(2)}, u32[]{:S(2)}) collective-permute-start(f32[2,1,16,128]{3,2,1,0:T(8,128)S(1)} %get-tuple-element.80), channel_id=1, source_target_pairs={{4,0},{8,4},{12,8},{0,12},{5,1},{9,5},{13,9},{1,13},{6,2},{10,6},{... | collective-permute-start | bytes 49160 | tf_op jit(solution)/shard_map/ppermute | solution.py:26
  54.8 9.8 %stack.363 = f32[1,8,2,8,2,64,2]{6,5,4,3,2,1,0:T(8,128)} reshape(f32[16,16,128]{2,1,0:T(8,128)S(1)} %get-tuple-element.119) | data formatting | bytes 262144 | tf_op jit(solution)/shard_map/stack | solution.py:38
  64.6 6.0 %copy.414 = f32[1,8,2,8,2,64,2]{5,3,6,4,2,1,0:T(8,128)} copy(f32[1,8,2,8,2,64,2]{6,5,4,3,2,1,0:T(8,128)} %stack.363) | data formatting | bytes 262144 | tf_op jit(solution)/shard_map/stack | solution.py:38
  71.4 1.8 collective-permute-start.37
  74.7 2.0 collective-permute-start.24
  79.9 2.2 collective-permute-done.25
  84.7 1.7 collective-permute-start.7
  89.0 3.8 %collective-permute-start.9 = (f32[2,1,16,128]{3,2,1,0:T(8,128)S(1)}, f32[2,1,16,128]{3,2,1,0:T(8,128)S(1)}, u32[]{:S(2)}, u32[]{:S(2)}) collective-permute-start(f32[2,1,16,128]{3,2,1,0:T(8,128)S(1)} %get-tuple-element.76), channel_id=1, source_target_pairs={{4,0},{8,4},{12,8},{0,12},{5,1},{9,5},{13,9},{1,13},{6,2},{10,6},{... | collective-permute-start | bytes 49160 | tf_op jit(solution)/shard_map/ppermute | solution.py:26
  97.9 1.7 collective-permute-start.15
  99.9 9.8 %stack.365 = f32[1,8,2,8,2,64,2]{6,5,4,3,2,1,0:T(8,128)} reshape(f32[16,16,128]{2,1,0:T(8,128)S(1)} %fusion.54) | data formatting | bytes 262144 | tf_op jit(solution)/shard_map/stack | solution.py:90
  109.7 5.5 %copy.419 = f32[1,8,2,8,2,64,2]{5,3,6,4,2,1,0:T(8,128)S(1)} copy(f32[1,8,2,8,2,64,2]{6,5,4,3,2,1,0:T(8,128)} %stack.365) | data formatting | bytes 262144 | tf_op jit(solution)/shard_map/stack | solution.py:90
  115.3 9.8 %stack.366 = f32[1,8,2,8,2,64,2]{6,5,4,3,2,1,0:T(8,128)} reshape(f32[16,16,128]{2,1,0:T(8,128)S(1)} %fusion.48) | data formatting | bytes 262144 | tf_op jit(solution)/shard_map/stack | solution.py:90
  125.2 5.5 %copy.420 = f32[1,8,2,8,2,64,2]{5,3,6,4,2,1,0:T(8,128)S(1)} copy(f32[1,8,2,8,2,64,2]{6,5,4,3,2,1,0:T(8,128)} %stack.366) | data formatting | bytes 262144 | tf_op jit(solution)/shard_map/stack | solution.py:90
  133.7 3.8 %collective-permute-start.17 = (f32[2,1,8,64]{3,2,1,0:T(8,128)S(1)}, f32[2,1,8,64]{3,2,1,0:T(8,128)S(1)}, u32[]{:S(2)}, u32[]{:S(2)}) collective-permute-start(f32[2,1,8,64]{3,2,1,0:T(8,128)S(1)} %get-tuple-element.173), channel_id=1, source_target_pairs={{4,0},{8,4},{12,8},{0,12},{5,1},{9,5},{13,9},{1,13},{6,2},{10,6},{... | collective-permute-start | bytes 12296 | tf_op jit(solution)/shard_map/ppermute | solution.py:26
  140.4 1.7 collective-permute-start.19
  142.8 3.0 mul.1078
  153.0 2.8 collective-permute-start.21
  157.5 1.7 collective-permute-start.23
  162.0 2.8 stack.377
  164.8 1.7 fusion.155
  166.5 2.8 stack.378
  169.4 2.0 fusion
  173.9 2.6 collective-permute-start.29
  183.5 2.6 collective-permute-start.33
  194.4 2.6 collective-permute-start.41
  203.4 2.6 collective-permute-start.45
  207.7 1.6 collective-permute-start.47
  212.4 2.6 collective-permute-start.49
  221.6 2.6 collective-permute-start.53
  230.6 2.6 collective-permute-start.57
  239.9 2.6 collective-permute-start.61
  249.0 2.6 collective-permute-start.65
  259.4 2.6 collective-permute-start.69
  268.7 2.6 collective-permute-start.73
  273.1 1.7 collective-permute-start.75
  283.7 2.6 collective-permute-start.77
  286.4 1.7 collective-permute-done.76
  288.4 1.7 collective-permute-start.79
  293.5 2.7 collective-permute-start.81
  296.4 1.7 collective-permute-done.80
  298.2 1.8 collective-permute-start.83
  (624 shorter events, 133.1 us)
Async XLA Ops:
  1.4 8.3 %collective-permute-start = (f32[2,1,16,128]{3,2,1,0:T(8,128)S(1)}, f32[2,1,16,128]{3,2,1,0:T(8,128)S(1)}, u32[]{:S(2)}, u32[]{:S(2)}) collective-permute-start(f32[2,1,16,128]{3,2,1,0:T(8,128)S(1)} %get-tuple-element.81), channel_id=1, source_target_pairs={{0,4},{4,8},{8,12},{12,0},{1,5},{5,9},{9,13},{13,1},{2,6},{6,10},{... | collective-permute-start | bytes 49160 | tf_op jit(solution)/shard_map/ppermute | solution.py:24
  4.5 5.3 %collective-permute-start.1 = (f32[2,1,16,128]{3,2,1,0:T(8,128)S(1)}, f32[2,1,16,128]{3,2,1,0:T(8,128)S(1)}, u32[]{:S(2)}, u32[]{:S(2)}) collective-permute-start(f32[2,1,16,128]{3,2,1,0:T(8,128)S(1)} %get-tuple-element.82), channel_id=1, source_target_pairs={{4,0},{8,4},{12,8},{0,12},{5,1},{9,5},{13,9},{1,13},{6,2},{10,6},{... | collective-permute-start | bytes 49160 | tf_op jit(solution)/shard_map/ppermute | solution.py:26
  10.8 17.8 %collective-permute-start.2 = (f32[2,18,1,128]{3,0,2,1:T(2,128)S(1)}, f32[2,18,1,128]{3,0,2,1:T(2,128)S(1)}, u32[]{:S(2)}, u32[]{:S(2)}) collective-permute-start(f32[2,18,1,128]{3,0,2,1:T(2,128)S(1)} %copy.455), channel_id=1, source_target_pairs={{0,1},{1,2},{2,3},{3,0},{4,5},{5,6},{6,7},{7,4},{8,9},{9,10},{10,1... | collective-permute-start | bytes 55304 | tf_op jit(solution)/shard_map/ppermute | solution.py:24
  10.8 17.8 %collective-permute-start.3 = (f32[2,18,1,128]{3,0,2,1:T(2,128)S(1)}, f32[2,18,1,128]{3,0,2,1:T(2,128)S(1)}, u32[]{:S(2)}, u32[]{:S(2)}) collective-permute-start(f32[2,18,1,128]{3,0,2,1:T(2,128)S(1)} %copy.456), channel_id=1, source_target_pairs={{1,0},{2,1},{3,2},{0,3},{5,4},{6,5},{7,6},{4,7},{9,8},{10,9},{11,1... | collective-permute-start | bytes 55304 | tf_op jit(solution)/shard_map/ppermute | solution.py:26
  51.0 31.8 %collective-permute-start.4 = (f32[2,1,16,128]{3,2,1,0:T(8,128)S(1)}, f32[2,1,16,128]{3,2,1,0:T(8,128)S(1)}, u32[]{:S(2)}, u32[]{:S(2)}) collective-permute-start(f32[2,1,16,128]{3,2,1,0:T(8,128)S(1)} %get-tuple-element.79), channel_id=1, source_target_pairs={{0,4},{4,8},{8,12},{12,0},{1,5},{5,9},{9,13},{13,1},{2,6},{6,10},{... | collective-permute-start | bytes 49160 | tf_op jit(solution)/shard_map/ppermute | solution.py:24
  51.0 32.3 %collective-permute-start.5 = (f32[2,1,16,128]{3,2,1,0:T(8,128)S(1)}, f32[2,1,16,128]{3,2,1,0:T(8,128)S(1)}, u32[]{:S(2)}, u32[]{:S(2)}) collective-permute-start(f32[2,1,16,128]{3,2,1,0:T(8,128)S(1)} %get-tuple-element.80), channel_id=1, source_target_pairs={{4,0},{8,4},{12,8},{0,12},{5,1},{9,5},{13,9},{1,13},{6,2},{10,6},{... | collective-permute-start | bytes 49160 | tf_op jit(solution)/shard_map/ppermute | solution.py:26
  70.6 14.0 %collective-permute-start.12 = (f32[1,8,64]{2,1,0:T(8,128)S(1)}, f32[1,8,64]{2,1,0:T(8,128)S(1)}, u32[]{:S(2)}, u32[]{:S(2)}) collective-permute-start(f32[1,8,64]{2,1,0:T(8,128)S(1)} %get-tuple-element.221), channel_id=1, source_target_pairs={{4,0},{8,4},{12,8},{0,12},{5,1},{9,5},{13,9},{1,13},{6,2},{10,6},{... | collective-permute-start | bytes 6152 | tf_op jit(solution)/shard_map/ppermute | solution.py:26
  71.4 5.4 %collective-permute-start.37 = (f32[1,2,16]{2,1,0:T(2,128)S(1)}, f32[1,2,16]{2,1,0:T(2,128)S(1)}, u32[]{:S(2)}, u32[]{:S(2)}) collective-permute-start(f32[1,2,16]{2,1,0:T(2,128)S(1)} %get-tuple-element.389), channel_id=1, source_target_pairs={{0,4},{4,8},{8,12},{12,0},{1,5},{5,9},{9,13},{13,1},{2,6},{6,10},{... | collective-permute-start | bytes 392 | tf_op jit(solution)/shard_map/ppermute | solution.py:24
  76.7 5.4 %collective-permute-start.25 = (f32[1,4,32]{2,1,0:T(4,128)S(1)}, f32[1,4,32]{2,1,0:T(4,128)S(1)}, u32[]{:S(2)}, u32[]{:S(2)}) collective-permute-start(f32[1,4,32]{2,1,0:T(4,128)S(1)} %get-tuple-element.311), channel_id=1, source_target_pairs={{0,4},{4,8},{8,12},{12,0},{1,5},{5,9},{9,13},{13,1},{2,6},{6,10},{... | collective-permute-start | bytes 1544 | tf_op jit(solution)/shard_map/ppermute | solution.py:24
  78.3 6.4 %collective-permute-start.13 = (f32[1,8,64]{2,1,0:T(8,128)S(1)}, f32[1,8,64]{2,1,0:T(8,128)S(1)}, u32[]{:S(2)}, u32[]{:S(2)}) collective-permute-start(f32[1,8,64]{2,1,0:T(8,128)S(1)} %get-tuple-element.220), channel_id=1, source_target_pairs={{0,4},{4,8},{8,12},{12,0},{1,5},{5,9},{9,13},{13,1},{2,6},{6,10},{... | collective-permute-start | bytes 6152 | tf_op jit(solution)/shard_map/ppermute | solution.py:24
  82.1 110.0 %collective-permute-start.38 = (f32[4,1,16]{2,1,0:T(1,128)}, f32[4,1,16]{2,1,0:T(1,128)}, u32[]{:S(2)}, u32[]{:S(2)}) collective-permute-start(f32[4,1,16]{2,1,0:T(1,128)} %get-tuple-element.343), channel_id=1, source_target_pairs={{1,0},{2,1},{3,2},{0,3},{5,4},{6,5},{7,6},{4,7},{9,8},{10,9},{11,1... | collective-permute-start | bytes 776 | tf_op jit(solution)/shard_map/ppermute | solution.py:26
  82.7 109.4 %collective-permute-start.39 = (f32[4,1,16]{2,1,0:T(1,128)}, f32[4,1,16]{2,1,0:T(1,128)}, u32[]{:S(2)}, u32[]{:S(2)}) collective-permute-start(f32[4,1,16]{2,1,0:T(1,128)} %get-tuple-element.342), channel_id=1, source_target_pairs={{0,1},{1,2},{2,3},{3,0},{4,5},{5,6},{6,7},{7,4},{8,9},{9,10},{10,1... | collective-permute-start | bytes 776 | tf_op jit(solution)/shard_map/ppermute | solution.py:24
  83.2 88.2 %collective-permute-start.26 = (f32[6,1,32]{2,1,0:T(1,128)}, f32[6,1,32]{2,1,0:T(1,128)}, u32[]{:S(2)}, u32[]{:S(2)}) collective-permute-start(f32[6,1,32]{2,1,0:T(1,128)} %get-tuple-element.263), channel_id=1, source_target_pairs={{1,0},{2,1},{3,2},{0,3},{5,4},{6,5},{7,6},{4,7},{9,8},{10,9},{11,1... | collective-permute-start | bytes 2312 | tf_op jit(solution)/shard_map/ppermute | solution.py:26
  88.9 5.6 %collective-permute-start.8 = (f32[2,1,16,128]{3,2,1,0:T(8,128)S(1)}, f32[2,1,16,128]{3,2,1,0:T(8,128)S(1)}, u32[]{:S(2)}, u32[]{:S(2)}) collective-permute-start(f32[2,1,16,128]{3,2,1,0:T(8,128)S(1)} %get-tuple-element.75), channel_id=1, source_target_pairs={{0,4},{4,8},{8,12},{12,0},{1,5},{5,9},{9,13},{13,1},{2,6},{6,10},{... | collective-permute-start | bytes 49160 | tf_op jit(solution)/shard_map/ppermute | solution.py:24
  89.0 5.5 %collective-permute-start.9 = (f32[2,1,16,128]{3,2,1,0:T(8,128)S(1)}, f32[2,1,16,128]{3,2,1,0:T(8,128)S(1)}, u32[]{:S(2)}, u32[]{:S(2)}) collective-permute-start(f32[2,1,16,128]{3,2,1,0:T(8,128)S(1)} %get-tuple-element.76), channel_id=1, source_target_pairs={{4,0},{8,4},{12,8},{0,12},{5,1},{9,5},{13,9},{1,13},{6,2},{10,6},{... | collective-permute-start | bytes 49160 | tf_op jit(solution)/shard_map/ppermute | solution.py:26
  97.8 33.0 %collective-permute-start.14 = (f32[10,1,64]{2,1,0:T(1,128)}, f32[10,1,64]{2,1,0:T(1,128)S(1)}, u32[]{:S(2)}, u32[]{:S(2)}) collective-permute-start(f32[10,1,64]{2,1,0:T(1,128)} %get-tuple-element.182), channel_id=1, source_target_pairs={{1,0},{2,1},{3,2},{0,3},{5,4},{6,5},{7,6},{4,7},{9,8},{10,9},{11,1... | collective-permute-start | bytes 7688 | tf_op jit(solution)/shard_map/ppermute | solution.py:26
  97.9 32.9 %collective-permute-start.15 = (f32[10,1,64]{2,1,0:T(1,128)}, f32[10,1,64]{2,1,0:T(1,128)S(1)}, u32[]{:S(2)}, u32[]{:S(2)}) collective-permute-start(f32[10,1,64]{2,1,0:T(1,128)} %get-tuple-element.183), channel_id=1, source_target_pairs={{0,1},{1,2},{2,3},{3,0},{4,5},{5,6},{6,7},{7,4},{8,9},{9,10},{10,1... | collective-permute-start | bytes 7688 | tf_op jit(solution)/shard_map/ppermute | solution.py:24
  133.7 5.5 %collective-permute-start.16 = (f32[2,1,8,64]{3,2,1,0:T(8,128)S(1)}, f32[2,1,8,64]{3,2,1,0:T(8,128)S(1)}, u32[]{:S(2)}, u32[]{:S(2)}) collective-permute-start(f32[2,1,8,64]{3,2,1,0:T(8,128)S(1)} %get-tuple-element.172), channel_id=1, source_target_pairs={{0,4},{4,8},{8,12},{12,0},{1,5},{5,9},{9,13},{13,1},{2,6},{6,10},{... | collective-permute-start | bytes 12296 | tf_op jit(solution)/shard_map/ppermute | solution.py:24
  133.7 5.5 %collective-permute-start.17 = (f32[2,1,8,64]{3,2,1,0:T(8,128)S(1)}, f32[2,1,8,64]{3,2,1,0:T(8,128)S(1)}, u32[]{:S(2)}, u32[]{:S(2)}) collective-permute-start(f32[2,1,8,64]{3,2,1,0:T(8,128)S(1)} %get-tuple-element.173), channel_id=1, source_target_pairs={{4,0},{8,4},{12,8},{0,12},{5,1},{9,5},{13,9},{1,13},{6,2},{10,6},{... | collective-permute-start | bytes 12296 | tf_op jit(solution)/shard_map/ppermute | solution.py:26
  139.8 6.1 %collective-permute-start.18 = (f32[2,10,1,64]{3,0,2,1:T(2,128)}, f32[2,10,1,64]{3,0,2,1:T(2,128)}, u32[]{:S(2)}, u32[]{:S(2)}) collective-permute-start(f32[2,10,1,64]{3,0,2,1:T(2,128)} %copy.457), channel_id=1, source_target_pairs={{0,1},{1,2},{2,3},{3,0},{4,5},{5,6},{6,7},{7,4},{8,9},{9,10},{10,1... | collective-permute-start | bytes 15368 | tf_op jit(solution)/shard_map/ppermute | solution.py:24
  140.4 6.2 %collective-permute-start.19 = (f32[2,10,1,64]{3,0,2,1:T(2,128)}, f32[2,10,1,64]{3,0,2,1:T(2,128)}, u32[]{:S(2)}, u32[]{:S(2)}) collective-permute-start(f32[2,10,1,64]{3,0,2,1:T(2,128)} %copy.458), channel_id=1, source_target_pairs={{1,0},{2,1},{3,2},{0,3},{5,4},{6,5},{7,6},{4,7},{9,8},{10,9},{11,1... | collective-permute-start | bytes 15368 | tf_op jit(solution)/shard_map/ppermute | solution.py:26
  151.9 5.5 %collective-permute-start.20 = (f32[2,1,8,64]{3,2,1,0:T(8,128)S(1)}, f32[2,1,8,64]{3,2,1,0:T(8,128)S(1)}, u32[]{:S(2)}, u32[]{:S(2)}) collective-permute-start(f32[2,1,8,64]{3,2,1,0:T(8,128)S(1)} %get-tuple-element.168), channel_id=1, source_target_pairs={{0,4},{4,8},{8,12},{12,0},{1,5},{5,9},{9,13},{13,1},{2,6},{6,10},{... | collective-permute-start | bytes 12296 | tf_op jit(solution)/shard_map/ppermute | solution.py:24
  153.0 4.3 %collective-permute-start.21 = (f32[2,1,8,64]{3,2,1,0:T(8,128)S(1)}, f32[2,1,8,64]{3,2,1,0:T(8,128)S(1)}, u32[]{:S(2)}, u32[]{:S(2)}) collective-permute-start(f32[2,1,8,64]{3,2,1,0:T(8,128)S(1)} %get-tuple-element.169), channel_id=1, source_target_pairs={{4,0},{8,4},{12,8},{0,12},{5,1},{9,5},{13,9},{1,13},{6,2},{10,6},{... | collective-permute-start | bytes 12296 | tf_op jit(solution)/shard_map/ppermute | solution.py:26
  160.5 10.9 %collective-permute-start.27 = (f32[6,1,32]{2,1,0:T(1,128)}, f32[6,1,32]{2,1,0:T(1,128)}, u32[]{:S(2)}, u32[]{:S(2)}) collective-permute-start(f32[6,1,32]{2,1,0:T(1,128)} %get-tuple-element.262), channel_id=1, source_target_pairs={{0,1},{1,2},{2,3},{3,0},{4,5},{5,6},{6,7},{7,4},{8,9},{9,10},{10,1... | collective-permute-start | bytes 2312 | tf_op jit(solution)/shard_map/ppermute | solution.py:24
  172.5 5.5 %collective-permute-start.28 = (f32[2,1,4,32]{3,2,1,0:T(4,128)S(1)}, f32[2,1,4,32]{3,2,1,0:T(4,128)S(1)}, u32[]{:S(2)}, u32[]{:S(2)}) collective-permute-start(f32[2,1,4,32]{3,2,1,0:T(4,128)S(1)} %get-tuple-element.260), channel_id=1, source_target_pairs={{0,4},{4,8},{8,12},{12,0},{1,5},{5,9},{9,13},{13,1},{2,6},{6,10},{... | collective-permute-start | bytes 3080 | tf_op jit(solution)/shard_map/ppermute | solution.py:24
  173.9 4.1 %collective-permute-start.29 = (f32[2,1,4,32]{3,2,1,0:T(4,128)S(1)}, f32[2,1,4,32]{3,2,1,0:T(4,128)S(1)}, u32[]{:S(2)}, u32[]{:S(2)}) collective-permute-start(f32[2,1,4,32]{3,2,1,0:T(4,128)S(1)} %get-tuple-element.261), channel_id=1, source_target_pairs={{4,0},{8,4},{12,8},{0,12},{5,1},{9,5},{13,9},{1,13},{6,2},{10,6},{... | collective-permute-start | bytes 3080 | tf_op jit(solution)/shard_map/ppermute | solution.py:26
  182.2 5.5 %collective-permute-start.32 = (f32[2,1,4,32]{3,2,1,0:T(4,128)S(1)}, f32[2,1,4,32]{3,2,1,0:T(4,128)S(1)}, u32[]{:S(2)}, u32[]{:S(2)}) collective-permute-start(f32[2,1,4,32]{3,2,1,0:T(4,128)S(1)} %get-tuple-element.256), channel_id=1, source_target_pairs={{0,4},{4,8},{8,12},{12,0},{1,5},{5,9},{9,13},{13,1},{2,6},{6,10},{... | collective-permute-start | bytes 3080 | tf_op jit(solution)/shard_map/ppermute | solution.py:24
  183.5 4.2 %collective-permute-start.33 = (f32[2,1,4,32]{3,2,1,0:T(4,128)S(1)}, f32[2,1,4,32]{3,2,1,0:T(4,128)S(1)}, u32[]{:S(2)}, u32[]{:S(2)}) collective-permute-start(f32[2,1,4,32]{3,2,1,0:T(4,128)S(1)} %get-tuple-element.257), channel_id=1, source_target_pairs={{4,0},{8,4},{12,8},{0,12},{5,1},{9,5},{13,9},{1,13},{6,2},{10,6},{... | collective-permute-start | bytes 3080 | tf_op jit(solution)/shard_map/ppermute | solution.py:26
  193.1 5.4 %collective-permute-start.40 = (f32[2,1,2,16]{3,2,1,0:T(2,128)S(1)}, f32[2,1,2,16]{3,2,1,0:T(2,128)S(1)}, u32[]{:S(2)}, u32[]{:S(2)}) collective-permute-start(f32[2,1,2,16]{3,2,1,0:T(2,128)S(1)} %get-tuple-element.340), channel_id=1, source_target_pairs={{0,4},{4,8},{8,12},{12,0},{1,5},{5,9},{9,13},{13,1},{2,6},{6,10},{... | collective-permute-start | bytes 776 | tf_op jit(solution)/shard_map/ppermute | solution.py:24
  194.4 4.1 %collective-permute-start.41 = (f32[2,1,2,16]{3,2,1,0:T(2,128)S(1)}, f32[2,1,2,16]{3,2,1,0:T(2,128)S(1)}, u32[]{:S(2)}, u32[]{:S(2)}) collective-permute-start(f32[2,1,2,16]{3,2,1,0:T(2,128)S(1)} %get-tuple-element.341), channel_id=1, source_target_pairs={{4,0},{8,4},{12,8},{0,12},{5,1},{9,5},{13,9},{1,13},{6,2},{10,6},{... | collective-permute-start | bytes 776 | tf_op jit(solution)/shard_map/ppermute | solution.py:26
  202.1 5.4 %collective-permute-start.44 = (f32[2,1,2,16]{3,2,1,0:T(2,128)S(1)}, f32[2,1,2,16]{3,2,1,0:T(2,128)S(1)}, u32[]{:S(2)}, u32[]{:S(2)}) collective-permute-start(f32[2,1,2,16]{3,2,1,0:T(2,128)S(1)} %get-tuple-element.336), channel_id=1, source_target_pairs={{0,4},{4,8},{8,12},{12,0},{1,5},{5,9},{9,13},{13,1},{2,6},{6,10},{... | collective-permute-start | bytes 776 | tf_op jit(solution)/shard_map/ppermute | solution.py:24
  203.4 4.1 %collective-permute-start.45 = (f32[2,1,2,16]{3,2,1,0:T(2,128)S(1)}, f32[2,1,2,16]{3,2,1,0:T(2,128)S(1)}, u32[]{:S(2)}, u32[]{:S(2)}) collective-permute-start(f32[2,1,2,16]{3,2,1,0:T(2,128)S(1)} %get-tuple-element.337), channel_id=1, source_target_pairs={{4,0},{8,4},{12,8},{0,12},{5,1},{9,5},{13,9},{1,13},{6,2},{10,6},{... | collective-permute-start | bytes 776 | tf_op jit(solution)/shard_map/ppermute | solution.py:26
  211.1 5.4 %collective-permute-start.48 = (f32[2,1,2,16]{3,2,1,0:T(2,128)S(1)}, f32[2,1,2,16]{3,2,1,0:T(2,128)S(1)}, u32[]{:S(2)}, u32[]{:S(2)}) collective-permute-start(f32[2,1,2,16]{3,2,1,0:T(2,128)S(1)} %get-tuple-element.332), channel_id=1, source_target_pairs={{0,4},{4,8},{8,12},{12,0},{1,5},{5,9},{9,13},{13,1},{2,6},{6,10},{... | collective-permute-start | bytes 776 | tf_op jit(solution)/shard_map/ppermute | solution.py:24
  212.4 4.1 %collective-permute-start.49 = (f32[2,1,2,16]{3,2,1,0:T(2,128)S(1)}, f32[2,1,2,16]{3,2,1,0:T(2,128)S(1)}, u32[]{:S(2)}, u32[]{:S(2)}) collective-permute-start(f32[2,1,2,16]{3,2,1,0:T(2,128)S(1)} %get-tuple-element.333), channel_id=1, source_target_pairs={{4,0},{8,4},{12,8},{0,12},{5,1},{9,5},{13,9},{1,13},{6,2},{10,6},{... | collective-permute-start | bytes 776 | tf_op jit(solution)/shard_map/ppermute | solution.py:26
  220.3 5.4 %collective-permute-start.52 = (f32[2,1,2,16]{3,2,1,0:T(2,128)S(1)}, f32[2,1,2,16]{3,2,1,0:T(2,128)S(1)}, u32[]{:S(2)}, u32[]{:S(2)}) collective-permute-start(f32[2,1,2,16]{3,2,1,0:T(2,128)S(1)} %get-tuple-element.328), channel_id=1, source_target_pairs={{0,4},{4,8},{8,12},{12,0},{1,5},{5,9},{9,13},{13,1},{2,6},{6,10},{... | collective-permute-start | bytes 776 | tf_op jit(solution)/shard_map/ppermute | solution.py:24
  229.3 5.4 %collective-permute-start.56 = (f32[2,1,2,16]{3,2,1,0:T(2,128)S(1)}, f32[2,1,2,16]{3,2,1,0:T(2,128)S(1)}, u32[]{:S(2)}, u32[]{:S(2)}) collective-permute-start(f32[2,1,2,16]{3,2,1,0:T(2,128)S(1)} %get-tuple-element.324), channel_id=1, source_target_pairs={{0,4},{4,8},{8,12},{12,0},{1,5},{5,9},{9,13},{13,1},{2,6},{6,10},{... | collective-permute-start | bytes 776 | tf_op jit(solution)/shard_map/ppermute | solution.py:24
  238.6 5.5 %collective-permute-start.60 = (f32[2,1,4,32]{3,2,1,0:T(4,128)S(1)}, f32[2,1,4,32]{3,2,1,0:T(4,128)S(1)}, u32[]{:S(2)}, u32[]{:S(2)}) collective-permute-start(f32[2,1,4,32]{3,2,1,0:T(4,128)S(1)} %get-tuple-element.242), channel_id=1, source_target_pairs={{0,4},{4,8},{8,12},{12,0},{1,5},{5,9},{9,13},{13,1},{2,6},{6,10},{... | collective-permute-start | bytes 3080 | tf_op jit(solution)/shard_map/ppermute | solution.py:24
  239.9 4.2 %collective-permute-start.61 = (f32[2,1,4,32]{3,2,1,0:T(4,128)S(1)}, f32[2,1,4,32]{3,2,1,0:T(4,128)S(1)}, u32[]{:S(2)}, u32[]{:S(2)}) collective-permute-start(f32[2,1,4,32]{3,2,1,0:T(4,128)S(1)} %get-tuple-element.243), channel_id=1, source_target_pairs={{4,0},{8,4},{12,8},{0,12},{5,1},{9,5},{13,9},{1,13},{6,2},{10,6},{... | collective-permute-start | bytes 3080 | tf_op jit(solution)/shard_map/ppermute | solution.py:26
  247.7 5.4 %collective-permute-start.64 = (f32[2,1,4,32]{3,2,1,0:T(4,128)S(1)}, f32[2,1,4,32]{3,2,1,0:T(4,128)S(1)}, u32[]{:S(2)}, u32[]{:S(2)}) collective-permute-start(f32[2,1,4,32]{3,2,1,0:T(4,128)S(1)} %get-tuple-element.238), channel_id=1, source_target_pairs={{0,4},{4,8},{8,12},{12,0},{1,5},{5,9},{9,13},{13,1},{2,6},{6,10},{... | collective-permute-start | bytes 3080 | tf_op jit(solution)/shard_map/ppermute | solution.py:24
  249.0 4.2 %collective-permute-start.65 = (f32[2,1,4,32]{3,2,1,0:T(4,128)S(1)}, f32[2,1,4,32]{3,2,1,0:T(4,128)S(1)}, u32[]{:S(2)}, u32[]{:S(2)}) collective-permute-start(f32[2,1,4,32]{3,2,1,0:T(4,128)S(1)} %get-tuple-element.239), channel_id=1, source_target_pairs={{4,0},{8,4},{12,8},{0,12},{5,1},{9,5},{13,9},{1,13},{6,2},{10,6},{... | collective-permute-start | bytes 3080 | tf_op jit(solution)/shard_map/ppermute | solution.py:26
  258.1 5.5 %collective-permute-start.68 = (f32[2,1,8,64]{3,2,1,0:T(8,128)S(1)}, f32[2,1,8,64]{3,2,1,0:T(8,128)S(1)}, u32[]{:S(2)}, u32[]{:S(2)}) collective-permute-start(f32[2,1,8,64]{3,2,1,0:T(8,128)S(1)} %get-tuple-element.164), channel_id=1, source_target_pairs={{0,4},{4,8},{8,12},{12,0},{1,5},{5,9},{9,13},{13,1},{2,6},{6,10},{... | collective-permute-start | bytes 12296 | tf_op jit(solution)/shard_map/ppermute | solution.py:24
  259.4 4.3 %collective-permute-start.69 = (f32[2,1,8,64]{3,2,1,0:T(8,128)S(1)}, f32[2,1,8,64]{3,2,1,0:T(8,128)S(1)}, u32[]{:S(2)}, u32[]{:S(2)}) collective-permute-start(f32[2,1,8,64]{3,2,1,0:T(8,128)S(1)} %get-tuple-element.165), channel_id=1, source_target_pairs={{4,0},{8,4},{12,8},{0,12},{5,1},{9,5},{13,9},{1,13},{6,2},{10,6},{... | collective-permute-start | bytes 12296 | tf_op jit(solution)/shard_map/ppermute | solution.py:26
  267.4 5.5 %collective-permute-start.72 = (f32[2,1,8,64]{3,2,1,0:T(8,128)S(1)}, f32[2,1,8,64]{3,2,1,0:T(8,128)S(1)}, u32[]{:S(2)}, u32[]{:S(2)}) collective-permute-start(f32[2,1,8,64]{3,2,1,0:T(8,128)S(1)} %get-tuple-element.160), channel_id=1, source_target_pairs={{0,4},{4,8},{8,12},{12,0},{1,5},{5,9},{9,13},{13,1},{2,6},{6,10},{... | collective-permute-start | bytes 12296 | tf_op jit(solution)/shard_map/ppermute | solution.py:24
  268.7 4.3 %collective-permute-start.73 = (f32[2,1,8,64]{3,2,1,0:T(8,128)S(1)}, f32[2,1,8,64]{3,2,1,0:T(8,128)S(1)}, u32[]{:S(2)}, u32[]{:S(2)}) collective-permute-start(f32[2,1,8,64]{3,2,1,0:T(8,128)S(1)} %get-tuple-element.161), channel_id=1, source_target_pairs={{4,0},{8,4},{12,8},{0,12},{5,1},{9,5},{13,9},{1,13},{6,2},{10,6},{... | collective-permute-start | bytes 12296 | tf_op jit(solution)/shard_map/ppermute | solution.py:26
  282.4 5.7 %collective-permute-start.76 = (f32[2,1,16,128]{3,2,1,0:T(8,128)S(1)}, f32[2,1,16,128]{3,2,1,0:T(8,128)S(1)}, u32[]{:S(2)}, u32[]{:S(2)}) collective-permute-start(f32[2,1,16,128]{3,2,1,0:T(8,128)S(1)} %get-tuple-element.71), channel_id=1, source_target_pairs={{0,4},{4,8},{8,12},{12,0},{1,5},{5,9},{9,13},{13,1},{2,6},{6,10},{... | collective-permute-start | bytes 49160 | tf_op jit(solution)/shard_map/ppermute | solution.py:24
  283.7 4.5 %collective-permute-start.77 = (f32[2,1,16,128]{3,2,1,0:T(8,128)S(1)}, f32[2,1,16,128]{3,2,1,0:T(8,128)S(1)}, u32[]{:S(2)}, u32[]{:S(2)}) collective-permute-start(f32[2,1,16,128]{3,2,1,0:T(8,128)S(1)} %get-tuple-element.72), channel_id=1, source_target_pairs={{4,0},{8,4},{12,8},{0,12},{5,1},{9,5},{13,9},{1,13},{6,2},{10,6},{... | collective-permute-start | bytes 49160 | tf_op jit(solution)/shard_map/ppermute | solution.py:26
  292.4 5.7 %collective-permute-start.80 = (f32[2,1,16,128]{3,2,1,0:T(8,128)S(1)}, f32[2,1,16,128]{3,2,1,0:T(8,128)S(1)}, u32[]{:S(2)}, u32[]{:S(2)}) collective-permute-start(f32[2,1,16,128]{3,2,1,0:T(8,128)S(1)} %get-tuple-element.67), channel_id=1, source_target_pairs={{0,4},{4,8},{8,12},{12,0},{1,5},{5,9},{9,13},{13,1},{2,6},{6,10},{... | collective-permute-start | bytes 49160 | tf_op jit(solution)/shard_map/ppermute | solution.py:24
  293.5 4.5 %collective-permute-start.81 = (f32[2,1,16,128]{3,2,1,0:T(8,128)S(1)}, f32[2,1,16,128]{3,2,1,0:T(8,128)S(1)}, u32[]{:S(2)}, u32[]{:S(2)}) collective-permute-start(f32[2,1,16,128]{3,2,1,0:T(8,128)S(1)} %get-tuple-element.68), channel_id=1, source_target_pairs={{4,0},{8,4},{12,8},{0,12},{5,1},{9,5},{13,9},{1,13},{6,2},{10,6},{... | collective-permute-start | bytes 49160 | tf_op jit(solution)/shard_map/ppermute | solution.py:26
  (109 other events, 1128.2 us)
where the time goes:
time: 304 us; the launch traced here: 303 us
  local copies, waits for them, and re-layouts  113 us (37%)
  starting transfers between devices  113 us (37%)
  waiting for transfers between devices  46.3 us (15%)
  other arithmetic  27.2 us (9%)
  between operations  3.25 us (1%)
    ppermute x42, starting transfers between devices, extended(): lax.ppermute(head, axis, [((i + 1) % count, i) for i in range(count)])  83.9 us
    ppermute x42, waiting for transfers between devices, extended(): lax.ppermute(tail, axis, [(i, (i + 1) % count) for i in range(count)])  43.1 us
    another operation x8, local copies, waits for them, and re-layouts, apply_operator(): return jnp.stack([first_eq, second_eq])  36.4 us
    another operation x4, local copies, waits for them, and re-layouts, right_of(): jnp.stack([concentration, concentration * concentration * concentration -...  31.7 us
    ppermute x42, starting transfers between devices, extended(): lax.ppermute(tail, axis, [(i, (i + 1) % count) for i in range(count)])  29.3 us
    slice x50, local copies, waits for them, and re-layouts, neighbour_list(): jnp.roll(middle, 1, axis=2)  13.5 us
    reshape x1, local copies, waits for them, and re-layouts, coarsen(): values.reshape(dims_now[:-3] + (dims_now[-3] // 2, 2, dims_now[-2] // 2,...  9.81 us
    reduce_sum x6, other arithmetic, coarsen(): return jnp.sum(grouped, axis=(-5, -3, -1)) * 0.125  6.47 us
  transfers between devices with their start and end apart: 84, of which 37 were waited for; matrix products, arithmetic and copies ran while one was open for 33% of the time, Pallas kernels for 0%

commit v1 on v0

--- a/solution.py
+++ b/solution.py
@@ -1,6 +1,10 @@
+import functools
+
 import jax
 import jax.numpy as jnp
 from jax import lax
+from jax.experimental import pallas as pl
+from jax.experimental.pallas import tpu as pltpu
 from jax.sharding import PartitionSpec as P
 
 LEVELS = 4
@@ -173,9 +177,372 @@
     return cycle_level(0, right_of(start_fields[0]))
 
 
+MESH = pl.DeviceIdType.MESH
+HALO = 4
+SIDES = (("lo", -1), ("hi", 1))
+CORNERS = ((-1, -1), (-1, 1), (1, -1), (1, 1))
+
+
+def iota(shape, dim):
+    return lax.broadcasted_iota(jnp.int32, shape, dim)
+
+
+def turn(values, shift, axis):
+    size = values.shape[axis]
+    return pltpu.roll(values, shift % size, axis)
+
+
+def near_sum(values, row_step, lane_step, wrap=False):
+    if wrap:
+        middle = values
+        total = jnp.concatenate([values[1:], values[:1]], 0) + jnp.concatenate(
+            [values[-1:], values[:-1]], 0
+        )
+    else:
+        middle = values[1:-1]
+        total = values[2:] + values[:-2]
+    total = total + (turn(middle, row_step, 1) + turn(middle, -row_step, 1))
+    return total + (turn(middle, lane_step, 2) + turn(middle, -lane_step, 2))
+
+
+def pair_sum(values, step, axis):
+    low = (iota(values.shape, axis) // step) % 2 == 0
+    return values + jnp.where(low, turn(values, -step, axis), turn(values, step, axis))
+
+
+def pair_rows(values):
+    grouped = values.reshape((values.shape[0] // 2, 2) + values.shape[1:])
+    return grouped[:, 0] + grouped[:, 1]
+
+
+def twice(values):
+    return jnp.concatenate([values[i // 2 : i // 2 + 1] for i in range(2 * values.shape[0])], 0)
+
+
+class Level:
+    def __init__(self, scale, mob, mob_sum, row_step, lane_step, wrap=False):
+        self.scale, self.mob = scale, mob
+        self.row_step, self.lane_step, self.wrap = row_step, lane_step, wrap
+        self.half = 0.5 * TIME_STEP * scale
+        self.diagonal = STABILIZER + 6.0 * GRADIENT_ENERGY * scale
+        self.coupling = self.half * (6.0 * mob + mob_sum)
+        self.damp = DAMPING / (1.0 + self.coupling * self.diagonal)
+
+    def part(self, values, size):
+        off = (values.shape[0] - size) // 2
+        return values[off : off + size]
+
+    def residual(self, conc, chem, right):
+        size = conc.shape[0] if self.wrap else conc.shape[0] - 2
+        sums = functools.partial(
+            near_sum, row_step=self.row_step, lane_step=self.lane_step, wrap=self.wrap
+        )
+        carried = self.part(self.mob, conc.shape[0]) * chem
+        mob = self.part(self.mob, size)
+        c, u = self.part(conc, size), self.part(chem, size)
+        first = (
+            self.part(right[0], size)
+            - c
+            + self.half * (mob * sums(chem) + sums(carried))
+            - self.part(self.coupling, size) * u
+        )
+        near = sums(conc) - 6.0 * c
+        second = (
+            self.part(right[1], size)
+            - u
+            + STABILIZER * c
+            - (GRADIENT_ENERGY * self.scale) * near
+        )
+        return first, second
+
+    def step(self, first, second):
+        size = first.shape[0]
+        damp = self.part(self.damp, size)
+        coupling = self.part(self.coupling, size)
+        return damp * (first - coupling * second), damp * (second + self.diagonal * first)
+
+    def sweep(self, conc, chem, right):
+        first, second = self.residual(conc, chem, right)
+        size = first.shape[0]
+        dc, du = self.step(first, second)
+        return self.part(conc, size) + dc, self.part(chem, size) + du
+
+
+def split_halves(first, second, first_high, second_high):
+    low = iota(first.shape, 1) < 4
+    first = turn(first, 4, 1) if first_high else first
+    second = second if second_high else turn(second, 4, 1)
+    return jnp.where(low, first, second)
+
+
+def cycle_kernel(nx, ny, conc_ref, chem_ref, conc_out, chem_out, *scratch):
+    (
+        edge0,
+        from_x0,
+        from_y0,
+        from_d0,
+        edge1,
+        whole1,
+        from_x1,
+        from_y1,
+        from_d1,
+        pack2,
+        grid2,
+        rows_buf,
+        send_sem,
+        recv_sem,
+    ) = scratch
+    img, gx, gy = lax.axis_index("img"), lax.axis_index("gx"), lax.axis_index("gy")
+
+    def at(dx, dy):
+        return (img, lax.rem(gx + dx + nx, nx), lax.rem(gy + dy + ny, ny))
+
+    peers = [(dx, dy) for dx in range(nx) for dy in range(ny) if (dx, dy) != (0, 0)]
+    barrier = pltpu.get_barrier_semaphore()
+    for dx, dy in peers:
+        pl.semaphore_signal(barrier, inc=1, device_id=at(dx, dy), device_id_type=MESH)
+
+    used = [0]
+    started = []
+
+    def send(src, dst, dx, dy):
+        index = used[0]
+        used[0] += 1
+        copy = pltpu.make_async_remote_copy(
+            src_ref=src,
+            dst_ref=dst,
+            send_sem=send_sem.at[index],
+            recv_sem=recv_sem.at[index],
+            device_id=at(dx, dy),
+            device_id_type=MESH,
+        )
+        copy.start()
+        started.append(copy)
+        return copy
+
+    size = conc_ref.shape[0]
+    conc, chem = conc_ref[...], chem_ref[...]
+    edge0[0] = split_halves(conc[:, :8], chem[:, :8], False, False)
+    edge0[1] = split_halves(conc[:, -8:], chem[:, -8:], True, True)
+    pl.semaphore_wait(barrier, len(peers))
+
+    waits = []
+    for side, dx in ((0, -1), (1, 1)):
+        rows = pl.ds(0, HALO) if dx < 0 else pl.ds(size - HALO, HALO)
+        waits.append(send(conc_ref.at[rows], from_x0.at[side, 0], dx, 0))
+        waits.append(send(chem_ref.at[rows], from_x0.at[side, 1], dx, 0))
+    for place, (dx, dy) in enumerate(CORNERS):
+        rows = pl.ds(0, HALO - 1) if dx < 0 else pl.ds(size - HALO + 1, HALO - 1)
+        waits.append(send(edge0.at[(dy + 1) // 2, rows], from_d0.at[place], dx, dy))
+    for side, dy in ((0, -1), (1, 1)):
+        waits.append(send(edge0.at[side], from_y0.at[side], 0, dy))
+    for copy in waits:
+        copy.wait_recv()
+
+    def halo_rows(center, corners):
+        lower, upper = corners[1], corners[0]
+        return jnp.concatenate([lower[:1], lower, center, upper, upper[:1]], 0)
+
+    def joined(right, left):
+        low = iota(right.shape, 1) < 4
+        return jnp.where(low, right, turn(left, 4, 1)), jnp.where(low, turn(right, 4, 1), left)
+
+    right0 = halo_rows(from_y0[0], (from_d0[0], from_d0[2]))
+    left0 = halo_rows(from_y0[1], (from_d0[1], from_d0[3]))
+    conc_halo, chem_halo = joined(right0, left0)
+    conc = jnp.concatenate([from_x0[1, 0], conc, from_x0[0, 0]], 0)
+    chem = jnp.concatenate([from_x0[1, 1], chem, from_x0[0, 1]], 0)
+    conc = jnp.concatenate([conc, conc_halo], 1)
+    chem = jnp.concatenate([chem, chem_halo], 1)
+
+    mob0 = mobility_of(conc)
+    level0 = Level(1.0, mob0[1:-1], near_sum(mob0, 1, 1), 1, 1)
+    level0.mob = mob0
+    right_side0 = (conc, conc * conc * conc - (1.0 + STABILIZER) * conc)
+
+    half = size // 2
+    mob_x = pair_sum(pair_rows(level0.part(mob0, size + 4)), 1, 2) * 0.125
+    rows_buf[: half + 2, :24] = mob_x
+    rows_buf[: half + 2, 24:32] = mob_x[:, 16:24]
+    mob1 = (
+        rows_buf[: half + 2, pl.ds(0, 16, stride=2)] + rows_buf[: half + 2, pl.ds(1, 16, stride=2)]
+    )
+    mob1_sum = near_sum(mob1, 1, 2)[:, :8]
+    mob1 = mob1[1:-1, :8]
+    even1 = iota((half, 8, 128), 2) % 2 == 0
+    whole1[1] = jnp.where(even1, mob1, mob1_sum)
+
+    conc, chem = level0.sweep(conc, chem, right_side0)
+    conc, chem = level0.sweep(conc, chem, right_side0)
+    fields0 = (conc, chem)
+    first, second = level0.residual(level0.part(conc, size + 2), level0.part(chem, size + 2), right_side0)
+
+    def coarse_right(values):
+        rows_buf[:half, :16] = pair_sum(pair_rows(values[:, :16]), 1, 2) * 0.125
+        return rows_buf[:half, pl.ds(0, 8, stride=2)] + rows_buf[:half, pl.ds(1, 8, stride=2)]
+
+    right_c = coarse_right(first)
+    right_u = coarse_right(second)
+    whole1[0] = jnp.where(even1, right_c, right_u)
+    edge1[0] = split_halves(whole1[0], whole1[1], False, False)
+    edge1[1] = split_halves(whole1[0], whole1[1], True, True)
+
+    waits = []
+    for side, dx in ((0, -1), (1, 1)):
+        rows = pl.ds(0, HALO) if dx < 0 else pl.ds(half - HALO, HALO)
+        waits.append(send(whole1.at[:, rows], from_x1.at[side], dx, 0))
+    for place, (dx, dy) in enumerate(CORNERS):
+        rows = pl.ds(0, HALO - 1) if dx < 0 else pl.ds(half - HALO + 1, HALO - 1)
+        waits.append(send(edge1.at[(dy + 1) // 2, rows], from_d1.at[place], dx, dy))
+    for side, dy in ((0, -1), (1, 1)):
+        waits.append(send(edge1.at[side], from_y1.at[side], 0, dy))
+    for copy in waits:
+        copy.wait_recv()
+
+    right1 = halo_rows(from_y1[0], (from_d1[0], from_d1[2]))
+    left1 = halo_rows(from_y1[1], (from_d1[1], from_d1[3]))
+    rhs_halo, mob_halo = joined(right1, left1)
+    rhs1 = jnp.concatenate([from_x1[1, 0], whole1[0], from_x1[0, 0]], 0)
+    mob1 = jnp.concatenate([from_x1[1, 1], whole1[1], from_x1[0, 1]], 0)
+    rhs1 = jnp.concatenate([rhs1, rhs_halo], 1)
+    mob1 = jnp.concatenate([mob1, mob_halo], 1)
+
+    def spread(values, step, axis):
+        low = (iota(values.shape, axis) // step) % 2 == 0
+        return (
+            jnp.where(low, values, turn(values, step, axis)),
+            jnp.where(low, turn(values, -step, axis), values),
+        )
+
+    rhs1 = spread(rhs1, 1, 2)
+    mob1, mob1_sum = spread(mob1, 1, 2)
+    level1 = Level(0.25, mob1, mob1_sum, 1, 2)
+    conc, chem = level1.step(*rhs1)
+    conc, chem = level1.sweep(conc, chem, rhs1)
+    fields1 = (conc, chem)
+    first, second = level1.residual(level1.part(conc, half + 2), level1.part(chem, half + 2), rhs1)
+
+    def coarse(values, row_step, lane_step):
+        return pair_sum(pair_sum(pair_rows(values), row_step, 1), lane_step, 2) * 0.125
+
+    quarter = half // 2
+    own = (
+        coarse(first[:, :8], 1, 2),
+        coarse(second[:, :8], 1, 2),
+        coarse(level1.part(mob1, half)[:, :8], 1, 2),
+    )
+
+    def by_lane(values):
+        lane = iota((8, 128), 1) % 4
+        return jnp.where(
+            lane < 2,
+            jnp.where(lane == 0, values[0], values[1]),
+            jnp.where(lane == 2, values[2], values[3]),
+        )
+
+    pack2[0] = jnp.where(iota((8, 128), 0) % 2 == 0, by_lane(own[0]), by_lane(own[1]))
+    pack2[1] = by_lane(own[2])
+    waits = []
+    for dx, dy in peers:
+        slot = grid2.at[(nx - dx) % nx, (ny - dy) % ny]
+        waits.append(send(pack2, slot, dx, dy))
+    grid2[0, 0] = pack2[...]
+    for copy in waits:
+        copy.wait_recv()
+
+    gathered = grid2[...]
+    rhs2 = gathered[:, :, 0].reshape(nx, ny * 8, 128)
+    mob2 = gathered[:, :, 1].reshape(nx, ny * 8, 128)
+
+    def by_row(values):
+        zero, one = spread(values, 1, 2)
+        zero, two = spread(zero, 2, 2)
+        one, three = spread(one, 2, 2)
+        together = jnp.stack([zero, one, two, three], 1)
+        return together.reshape((nx * quarter,) + values.shape[1:])
+
+    rhs2 = tuple(by_row(v) for v in spread(rhs2, 1, 1))
+    mob2 = by_row(mob2)
+    level2 = Level(0.0625, mob2, near_sum(mob2, 2, 4, True), 2, 4, True)
+    mob3 = coarse(mob2, 2, 4)
+    level3 = Level(0.015625, mob3, near_sum(mob3, 4, 8, True), 4, 8, True)
+
+    conc, chem = level2.step(*rhs2)
+    conc, chem = level2.sweep(conc, chem, rhs2)
+    rhs3 = tuple(coarse(v, 2, 4) for v in level2.residual(conc, chem, rhs2))
+    low_conc, low_chem = level3.step(*rhs3)
+    for _ in range(COARSE - 1):
+        low_conc, low_chem = level3.sweep(low_conc, low_chem, rhs3)
+    conc, chem = conc + twice(low_conc), chem + twice(low_chem)
+    for _ in range(SWEEPS):
+        conc, chem = level2.sweep(conc, chem, rhs2)
+
+    def around1(values):
+        values = jnp.concatenate([values[-2:], values[: quarter + 2]], 0)
+        low = iota((quarter + 4, 8, 128), 1) < 4
+        beside = jnp.where(low, values[:, 8:16], values[:, -8:])
+        return twice(jnp.concatenate([values[:, :8], beside], 1))[1:-1]
+
+    conc, chem = fields1[0] + around1(conc), fields1[1] + around1(chem)
+    for _ in range(SWEEPS):
+        conc, chem = level1.sweep(conc, chem, rhs1)
+
+    def around0(values):
+        count = values.shape[0]
+        rows_buf[:count, pl.ds(0, 16, stride=2)] = values
+        rows_buf[:count, pl.ds(1, 16, stride=2)] = values
+        doubled = rows_buf[:count]
+        low = iota((count, 8, 128), 1) < 4
+        beside = jnp.where(low, doubled[:, 16:24], doubled[:, 24:32])
+        return twice(jnp.concatenate([doubled[:, :16], beside], 1))
+
+    conc, chem = fields0[0] + around0(conc), fields0[1] + around0(chem)
+    for _ in range(SWEEPS):
+        conc, chem = level0.sweep(conc, chem, right_side0)
+    conc_out[...] = conc[:, :16]
+    chem_out[...] = chem[:, :16]
+    for copy in started:
+        copy.wait_send()
+
+
+def gathered_cycle(nx, ny, conc_old, chem_old):
+    size = conc_old.shape[0]
+    half = size // 2
+    copies = 18 + nx * ny - 1
+    scratch = [
+        (2, size, 8, 128),
+        (2, 2, HALO, 16, 128),
+        (2, size, 8, 128),
+        (4, HALO - 1, 8, 128),
+        (2, half, 8, 128),
+        (2, half, 8, 128),
+        (2, 2, HALO, 8, 128),
+        (2, half, 8, 128),
+        (4, HALO - 1, 8, 128),
+        (2, 8, 128),
+        (nx, ny, 2, 8, 128),
+        (half + 2, 32, 128),
+    ]
+    shape = jax.ShapeDtypeStruct(conc_old.shape, jnp.float32)
+    space = pl.BlockSpec(memory_space=pltpu.VMEM)
+    return pl.pallas_call(
+        functools.partial(cycle_kernel, nx, ny),
+        out_shape=(shape, shape),
+        in_specs=[space, space],
+        out_specs=(space, space),
+        scratch_shapes=[pltpu.VMEM(dims, jnp.float32) for dims in scratch]
+        + [pltpu.SemaphoreType.DMA((copies,)), pltpu.SemaphoreType.DMA((copies,))],
+        compiler_params=pltpu.CompilerParams(
+            collective_id=0, has_side_effects=True, vmem_limit_bytes=32 * 1024 * 1024
+        ),
+    )(conc_old, chem_old)
+
+
 def body(conc_old, chem_old):
-    start_fields = jnp.stack([conc_old, chem_old])
-    result = plain_solve(start_fields)
+    nx, ny = lax.axis_size("gx"), lax.axis_size("gy")
+    if conc_old.shape == (16, 16, 128) and min(nx, ny) >= 3 and nx * ny <= 16:
+        return gathered_cycle(nx, ny, conc_old, chem_old)
+    result = plain_solve(jnp.stack([conc_old, chem_old]))
     return (result[0], result[1])
 
 

time: 304 us -> 34.1 us (0.11)
  starting transfers between devices: 113 us -> 0 us
  local copies, waits for them, and re-layouts: 113 us -> 3.11 us
  waiting for transfers between devices: 46.3 us -> 0 us
  Pallas kernels: 0 us -> 30.2 us
  other arithmetic: 27.2 us -> 0 us
    ppermute x84 -> x0, starting transfers between devices: 113 us -> none  [the longest x42 83.9 us: extended(): lax.ppermute(head, axis, [((i + 1) % count, i) for i in range(count)])]
    another operation x12 -> x0, local copies, waits for them, and re-layouts: 68.1 us -> none  [the longest x8 36.4 us: apply_operator(): return jnp.stack([first_eq, second_eq])]
    ppermute x84 -> x0, waiting for transfers between devices: 46.3 us -> none  [the longest x42 43.1 us: extended(): lax.ppermute(tail, axis, [(i, (i + 1) % count) for i in range(count)])]
    pallas_call x0 -> x1, Pallas kernels: none -> 30.2 us  [gathered_cycle(): pl.pallas_call(functools.partial(cycle_kernel, nx, ny), out_shape=(shape,...]
    slice x113 -> x0, local copies, waits for them, and re-layouts: 20 us -> none  [the longest x50 13.5 us: neighbour_list(): jnp.roll(middle, 1, axis=2)]
    reshape x7 -> x0, local copies, waits for them, and re-layouts: 13.3 us -> none  [the longest x1 9.81 us: coarsen(): values.reshape(dims_now[:-3] + (dims_now[-3] // 2, 2, dims_now[-2] // 2,...]
    another operation x52 -> x0, other arithmetic: 8.69 us -> none  [the longest x29 5.27 us: apply_operator(): return jnp.stack([first_eq, second_eq])]
    reduce_sum x6 -> x0, other arithmetic: 6.47 us -> none  [coarsen(): return jnp.sum(grouped, axis=(-5, -3, -1)) * 0.125]
  transfers between devices with their start and end apart: 84 -> 0, of which waited for: 37 -> 0; matrix products, arithmetic and copies ran while one was open for 33% -> 0% of each run, Pallas kernels for 0% -> 0%
where the time goes in v1:
time: 34.1 us; the launch traced here: 33.9 us
  Pallas kernels  30.2 us (89%)
  local copies, waits for them, and re-layouts  3.11 us (9%)
  between operations  0.65 us (2%)
    pallas_call x1, Pallas kernels, gathered_cycle(): pl.pallas_call(functools.partial(cycle_kernel, nx, ny), out_shape=(shape,...  30.2 us
    unnamed x6, local copies, waits for them, and re-layouts  3.11 us

profile of v1, /device:TPU:0, one launch (start us, length us, event | category | flops | bytes accessed | tf_op | source)
XLA Modules:
  0.0 33.9 jit_solution(3467969193207811875)
XLA Ops:
  0.6 0.0 copy-start
  0.6 0.9 %copy-done = f32[16,16,128]{2,1,0:T(8,128)S(1)} copy-done((f32[16,16,128]{2,1,0:T(8,128)S(1)}, f32[16,16,128]{2,1,0:T(8,128)}, u32[]{:S(2)}) %copy-start) | copy-done | bytes 131096
  1.5 0.0 copy-start.1
  1.5 0.9 %copy-done.1 = f32[16,16,128]{2,1,0:T(8,128)S(1)} copy-done((f32[16,16,128]{2,1,0:T(8,128)S(1)}, f32[16,16,128]{2,1,0:T(8,128)}, u32[]{:S(2)}) %copy-start.1) | copy-done | bytes 131096
  2.4 30.2 %shard_map.41 = (f32[16,16,128]{2,1,0:T(8,128)S(1)}, f32[16,16,128]{2,1,0:T(8,128)S(1)}) custom-call(f32[16,16,128]{2,1,0:T(8,128)S(1)} %copy-done, f32[16,16,128]{2,1,0:T(8,128)S(1)} %copy-done.1), custom_call_target="tpu_custom_call" | custom-call | tf_op jit(solution)/shard_map/pallas_call | solution.py:528
  32.6 0.7 %copy.6 = f32[16,16,128]{2,1,0:T(8,128)} copy(f32[16,16,128]{2,1,0:T(8,128)S(1)} %get-tuple-element.4) | data formatting | bytes 262144
  33.3 0.7 %copy.7 = f32[16,16,128]{2,1,0:T(8,128)} copy(f32[16,16,128]{2,1,0:T(8,128)S(1)} %get-tuple-element.5) | data formatting | bytes 262144
Async XLA Ops:
  0.6 0.9 %copy-start = (f32[16,16,128]{2,1,0:T(8,128)S(1)}, f32[16,16,128]{2,1,0:T(8,128)}, u32[]{:S(2)}) copy-start(f32[16,16,128]{2,1,0:T(8,128)} %conc_ref.1) | copy-start | bytes 393220
  1.5 0.9 %copy-start.1 = (f32[16,16,128]{2,1,0:T(8,128)S(1)}, f32[16,16,128]{2,1,0:T(8,128)}, u32[]{:S(2)}) copy-start(f32[16,16,128]{2,1,0:T(8,128)} %chem_ref.1) | copy-start | bytes 393220

commit v2 on v1

--- a/solution.py
+++ b/solution.py
@@ -277,22 +277,31 @@
 
 def cycle_kernel(nx, ny, conc_ref, chem_ref, conc_out, chem_out, *scratch):
     (
+        own_conc,
+        own_chem,
         edge0,
         from_x0,
         from_y0,
         from_d0,
+        whole1,
         edge1,
-        whole1,
         from_x1,
         from_y1,
         from_d1,
         pack2,
         grid2,
         rows_buf,
+        load_sem,
         send_sem,
         recv_sem,
     ) = scratch
     img, gx, gy = lax.axis_index("img"), lax.axis_index("gx"), lax.axis_index("gy")
+    loads = [
+        pltpu.make_async_copy(conc_ref, own_conc, load_sem.at[0]),
+        pltpu.make_async_copy(chem_ref, own_chem, load_sem.at[1]),
+    ]
+    for load in loads:
+        load.start()
 
     def at(dx, dy):
         return (img, lax.rem(gx + dx + nx, nx), lax.rem(gy + dy + ny, ny))
@@ -320,8 +329,16 @@
         started.append(copy)
         return copy
 
-    size = conc_ref.shape[0]
-    conc, chem = conc_ref[...], chem_ref[...]
+    def arrive(copies):
+        for copy in copies:
+            copy.wait_recv()
+
+    for load in loads:
+        load.wait()
+    size = own_conc.shape[0]
+    half = size // 2
+    quarter = half // 2
+    conc, chem = own_conc[...], own_chem[...]
     edge0[0] = split_halves(conc[:, :8], chem[:, :8], False, False)
     edge0[1] = split_halves(conc[:, -8:], chem[:, -8:], True, True)
     pl.semaphore_wait(barrier, len(peers))
@@ -329,83 +346,46 @@
     waits = []
     for side, dx in ((0, -1), (1, 1)):
         rows = pl.ds(0, HALO) if dx < 0 else pl.ds(size - HALO, HALO)
-        waits.append(send(conc_ref.at[rows], from_x0.at[side, 0], dx, 0))
-        waits.append(send(chem_ref.at[rows], from_x0.at[side, 1], dx, 0))
+        waits.append(send(own_conc.at[rows], from_x0.at[side, 0], dx, 0))
+        waits.append(send(own_chem.at[rows], from_x0.at[side, 1], dx, 0))
     for place, (dx, dy) in enumerate(CORNERS):
         rows = pl.ds(0, HALO - 1) if dx < 0 else pl.ds(size - HALO + 1, HALO - 1)
         waits.append(send(edge0.at[(dy + 1) // 2, rows], from_d0.at[place], dx, dy))
     for side, dy in ((0, -1), (1, 1)):
         waits.append(send(edge0.at[side], from_y0.at[side], 0, dy))
-    for copy in waits:
-        copy.wait_recv()
-
-    def halo_rows(center, corners):
-        lower, upper = corners[1], corners[0]
-        return jnp.concatenate([lower[:1], lower, center, upper, upper[:1]], 0)
+    arrive(waits)
+
+    def halo_rows(center, lower, upper):
+        return jnp.concatenate([lower[:1], lower, center, upper, upper[-1:]], 0)
 
     def joined(right, left):
         low = iota(right.shape, 1) < 4
         return jnp.where(low, right, turn(left, 4, 1)), jnp.where(low, turn(right, 4, 1), left)
 
-    right0 = halo_rows(from_y0[0], (from_d0[0], from_d0[2]))
-    left0 = halo_rows(from_y0[1], (from_d0[1], from_d0[3]))
+    right0 = halo_rows(from_y0[0], from_d0[2], from_d0[0])
+    left0 = halo_rows(from_y0[1], from_d0[3], from_d0[1])
     conc_halo, chem_halo = joined(right0, left0)
     conc = jnp.concatenate([from_x0[1, 0], conc, from_x0[0, 0]], 0)
     chem = jnp.concatenate([from_x0[1, 1], chem, from_x0[0, 1]], 0)
     conc = jnp.concatenate([conc, conc_halo], 1)
     chem = jnp.concatenate([chem, chem_halo], 1)
 
-    mob0 = mobility_of(conc)
-    level0 = Level(1.0, mob0[1:-1], near_sum(mob0, 1, 1), 1, 1)
-    level0.mob = mob0
-    right_side0 = (conc, conc * conc * conc - (1.0 + STABILIZER) * conc)
-
-    half = size // 2
-    mob_x = pair_sum(pair_rows(level0.part(mob0, size + 4)), 1, 2) * 0.125
-    rows_buf[: half + 2, :24] = mob_x
-    rows_buf[: half + 2, 24:32] = mob_x[:, 16:24]
-    mob1 = (
-        rows_buf[: half + 2, pl.ds(0, 16, stride=2)] + rows_buf[: half + 2, pl.ds(1, 16, stride=2)]
-    )
-    mob1_sum = near_sum(mob1, 1, 2)[:, :8]
-    mob1 = mob1[1:-1, :8]
-    even1 = iota((half, 8, 128), 2) % 2 == 0
-    whole1[1] = jnp.where(even1, mob1, mob1_sum)
-
-    conc, chem = level0.sweep(conc, chem, right_side0)
-    conc, chem = level0.sweep(conc, chem, right_side0)
-    fields0 = (conc, chem)
-    first, second = level0.residual(level0.part(conc, size + 2), level0.part(chem, size + 2), right_side0)
-
-    def coarse_right(values):
-        rows_buf[:half, :16] = pair_sum(pair_rows(values[:, :16]), 1, 2) * 0.125
-        return rows_buf[:half, pl.ds(0, 8, stride=2)] + rows_buf[:half, pl.ds(1, 8, stride=2)]
-
-    right_c = coarse_right(first)
-    right_u = coarse_right(second)
-    whole1[0] = jnp.where(even1, right_c, right_u)
-    edge1[0] = split_halves(whole1[0], whole1[1], False, False)
-    edge1[1] = split_halves(whole1[0], whole1[1], True, True)
-
-    waits = []
-    for side, dx in ((0, -1), (1, 1)):
-        rows = pl.ds(0, HALO) if dx < 0 else pl.ds(half - HALO, HALO)
-        waits.append(send(whole1.at[:, rows], from_x1.at[side], dx, 0))
-    for place, (dx, dy) in enumerate(CORNERS):
-        rows = pl.ds(0, HALO - 1) if dx < 0 else pl.ds(half - HALO + 1, HALO - 1)
-        waits.append(send(edge1.at[(dy + 1) // 2, rows], from_d1.at[place], dx, dy))
-    for side, dy in ((0, -1), (1, 1)):
-        waits.append(send(edge1.at[side], from_y1.at[side], 0, dy))
-    for copy in waits:
-        copy.wait_recv()
-
-    right1 = halo_rows(from_y1[0], (from_d1[0], from_d1[2]))
-    left1 = halo_rows(from_y1[1], (from_d1[1], from_d1[3]))
-    rhs_halo, mob_halo = joined(right1, left1)
-    rhs1 = jnp.concatenate([from_x1[1, 0], whole1[0], from_x1[0, 0]], 0)
-    mob1 = jnp.concatenate([from_x1[1, 1], whole1[1], from_x1[0, 1]], 0)
-    rhs1 = jnp.concatenate([rhs1, rhs_halo], 1)
-    mob1 = jnp.concatenate([mob1, mob_halo], 1)
+    def row_pairs(values):
+        count, rows = values.shape[:2]
+        rows_buf[:count, :rows] = values
+        return (
+            rows_buf[:count, pl.ds(0, rows // 2, stride=2)]
+            + rows_buf[:count, pl.ds(1, rows // 2, stride=2)]
+        )
+
+    def rows_twice(values):
+        count, rows = values.shape[:2]
+        rows_buf[:count, pl.ds(0, rows, stride=2)] = values
+        rows_buf[:count, pl.ds(1, rows, stride=2)] = values
+        return rows_buf[:count, : 2 * rows]
+
+    def coarse(values, lane_step):
+        return row_pairs(pair_sum(pair_rows(values), lane_step, 2) * 0.125)
 
     def spread(values, step, axis):
         low = (iota(values.shape, axis) // step) % 2 == 0
@@ -413,24 +393,6 @@
             jnp.where(low, values, turn(values, step, axis)),
             jnp.where(low, turn(values, -step, axis), values),
         )
-
-    rhs1 = spread(rhs1, 1, 2)
-    mob1, mob1_sum = spread(mob1, 1, 2)
-    level1 = Level(0.25, mob1, mob1_sum, 1, 2)
-    conc, chem = level1.step(*rhs1)
-    conc, chem = level1.sweep(conc, chem, rhs1)
-    fields1 = (conc, chem)
-    first, second = level1.residual(level1.part(conc, half + 2), level1.part(chem, half + 2), rhs1)
-
-    def coarse(values, row_step, lane_step):
-        return pair_sum(pair_sum(pair_rows(values), row_step, 1), lane_step, 2) * 0.125
-
-    quarter = half // 2
-    own = (
-        coarse(first[:, :8], 1, 2),
-        coarse(second[:, :8], 1, 2),
-        coarse(level1.part(mob1, half)[:, :8], 1, 2),
-    )
 
     def by_lane(values):
         lane = iota((8, 128), 1) % 4
@@ -440,19 +402,98 @@
             jnp.where(lane == 2, values[2], values[3]),
         )
 
+    def twice_pair(values):
+        return pair_sum(values, 1, 1)
+
+    def gather(kind):
+        copies = []
+        for dx, dy in peers:
+            rows = pl.ds(8 * ((ny - dy) % ny), 8)
+            copies.append(send(pack2.at[kind], grid2.at[kind, (nx - dx) % nx, rows], dx, dy))
+        grid2[kind, 0, :8] = pack2[kind]
+        return copies
+
+    def swap1(kind, inner):
+        first, rest = [], []
+        edge1[kind, 0] = split_halves(whole1[kind, :4], whole1[kind, 4:], False, False)
+        edge1[kind, 1] = split_halves(whole1[kind, :4], whole1[kind, 4:], True, True)
+
+        def move(copies, src, dst, start, count, dx, dy, shift=0):
+            if count > 0:
+                source = src.at[pl.ds(start + shift, count)]
+                copies.append(send(source, dst.at[pl.ds(start, count)], dx, dy))
+
+        for copies in (first, rest):
+            near = copies is first
+            for side, dx in ((0, -1), (1, 1)):
+                count = inner if near else HALO - inner
+                start = 0 if (dx < 0) == near else HALO - count
+                shift = 0 if dx < 0 else half - HALO
+                move(copies, whole1.at[kind], from_x1.at[kind, side], start, count, dx, 0, shift)
+            for place, (dx, dy) in enumerate(CORNERS):
+                count = inner - 1 if near else HALO - inner
+                if dx < 0:
+                    start = 0 if near else inner - 1
+                else:
+                    start = HALO - inner + 1 if near else 1
+                source = edge1.at[kind, (dy + 1) // 2]
+                move(copies, source, from_d1.at[kind, place], start, count, dx, dy)
+            if near:
+                for side, dy in ((0, -1), (1, 1)):
+                    copies.append(send(edge1.at[kind, side], from_y1.at[kind, side], 0, dy))
+        return first, rest
+
+    def padded1(kind, width):
+        below, above = pl.ds(HALO - width + 1, width - 1), pl.ds(0, width - 1)
+        lower = joined(from_d1[kind, 2, below], from_d1[kind, 3, below])[1]
+        upper = joined(from_d1[kind, 0, above], from_d1[kind, 1, above])[0]
+        center = jnp.concatenate(joined(from_y1[kind, 0], from_y1[kind, 1]), 0)
+        inside = [from_x1[kind, 1, HALO - width :], whole1[kind], from_x1[kind, 0, :width]]
+        return jnp.concatenate(
+            [jnp.concatenate(inside, 0), halo_rows(center, lower, upper)], 1
+        )
+
+    mob0 = mobility_of(conc)
+    mob_x = pair_sum(pair_rows(mob0[2:-2]), 1, 2) * 0.125
+    mob1 = row_pairs(jnp.concatenate([mob_x, mob_x[:, 16:24]], 1))
+    mob1_sum = near_sum(mob1, 1, 2)[:, :8]
+    mob1 = mob1[1:-1, :8]
+    even1 = iota((half, 8, 128), 2) % 2 == 0
+    whole1[1] = jnp.where(even1, mob1, mob1_sum)
+    mob1_waits, _ = swap1(1, HALO)
+    pack2[1] = by_lane(twice_pair(pair_sum(pair_rows(mob1), 2, 2) * 0.125))
+    mob2_waits = gather(1)
+
+    level0 = Level(1.0, mob0[1:-1], near_sum(mob0, 1, 1), 1, 1)
+    level0.mob = mob0
+    right_side0 = (conc, conc * conc * conc - (1.0 + STABILIZER) * conc)
+    conc, chem = level0.sweep(conc, chem, right_side0)
+    conc, chem = level0.sweep(conc, chem, right_side0)
+    fields0 = (conc, chem)
+    first, second = level0.residual(
+        level0.part(conc, size + 2), level0.part(chem, size + 2), right_side0
+    )
+    whole1[0] = jnp.where(even1, coarse(first[:, :16], 1), coarse(second[:, :16], 1))
+    near_waits, far_waits = swap1(0, 2)
+
+    arrive(mob1_waits)
+    mob1, mob1_sum = spread(padded1(1, HALO), 1, 2)
+    level1 = Level(0.25, mob1, mob1_sum, 1, 2)
+    arrive(near_waits)
+    rhs1 = spread(padded1(0, 2), 1, 2)
+    conc, chem = level1.step(*rhs1)
+    conc, chem = level1.sweep(conc, chem, rhs1)
+    own = [
+        twice_pair(pair_sum(pair_rows(values[:, :8]), 2, 2) * 0.125)
+        for values in level1.residual(conc, chem, rhs1)
+    ]
     pack2[0] = jnp.where(iota((8, 128), 0) % 2 == 0, by_lane(own[0]), by_lane(own[1]))
-    pack2[1] = by_lane(own[2])
-    waits = []
-    for dx, dy in peers:
-        slot = grid2.at[(nx - dx) % nx, (ny - dy) % ny]
-        waits.append(send(pack2, slot, dx, dy))
-    grid2[0, 0] = pack2[...]
-    for copy in waits:
-        copy.wait_recv()
-
-    gathered = grid2[...]
-    rhs2 = gathered[:, :, 0].reshape(nx, ny * 8, 128)
-    mob2 = gathered[:, :, 1].reshape(nx, ny * 8, 128)
+    rhs2_waits = gather(0)
+
+    arrive(far_waits)
+    rhs1 = spread(padded1(0, HALO), 1, 2)
+    conc, chem = level1.step(*rhs1)
+    fields1 = level1.sweep(conc, chem, rhs1)
 
     def by_row(values):
         zero, one = spread(values, 1, 2)
@@ -461,24 +502,28 @@
         together = jnp.stack([zero, one, two, three], 1)
         return together.reshape((nx * quarter,) + values.shape[1:])
 
-    rhs2 = tuple(by_row(v) for v in spread(rhs2, 1, 1))
-    mob2 = by_row(mob2)
-    level2 = Level(0.0625, mob2, near_sum(mob2, 2, 4, True), 2, 4, True)
-    mob3 = coarse(mob2, 2, 4)
-    level3 = Level(0.015625, mob3, near_sum(mob3, 4, 8, True), 4, 8, True)
-
+    arrive(mob2_waits)
+    mob2 = by_row(grid2[1, :, pl.ds(0, 4 * ny, stride=2)])
+    level2 = Level(0.0625, mob2, near_sum(mob2, 1, 4, True), 1, 4, True)
+    mob3 = coarse(mob2, 4)
+    level3 = Level(0.015625, mob3, near_sum(mob3, 1, 8, True), 1, 8, True)
+
+    arrive(rhs2_waits)
+    rhs2 = [by_row(grid2[0, :, pl.ds(start, 4 * ny, stride=2)]) for start in (0, 1)]
     conc, chem = level2.step(*rhs2)
     conc, chem = level2.sweep(conc, chem, rhs2)
-    rhs3 = tuple(coarse(v, 2, 4) for v in level2.residual(conc, chem, rhs2))
+    rhs3 = [coarse(v, 4) for v in level2.residual(conc, chem, rhs2)]
     low_conc, low_chem = level3.step(*rhs3)
     for _ in range(COARSE - 1):
         low_conc, low_chem = level3.sweep(low_conc, low_chem, rhs3)
-    conc, chem = conc + twice(low_conc), chem + twice(low_chem)
+    conc = conc + twice(rows_twice(low_conc))
+    chem = chem + twice(rows_twice(low_chem))
     for _ in range(SWEEPS):
         conc, chem = level2.sweep(conc, chem, rhs2)
 
     def around1(values):
         values = jnp.concatenate([values[-2:], values[: quarter + 2]], 0)
+        values = rows_twice(values)
         low = iota((quarter + 4, 8, 128), 1) < 4
         beside = jnp.where(low, values[:, 8:16], values[:, -8:])
         return twice(jnp.concatenate([values[:, :8], beside], 1))[1:-1]
@@ -488,11 +533,8 @@
         conc, chem = level1.sweep(conc, chem, rhs1)
 
     def around0(values):
-        count = values.shape[0]
-        rows_buf[:count, pl.ds(0, 16, stride=2)] = values
-        rows_buf[:count, pl.ds(1, 16, stride=2)] = values
-        doubled = rows_buf[:count]
-        low = iota((count, 8, 128), 1) < 4
+        doubled = rows_twice(values)
+        low = iota((values.shape[0], 8, 128), 1) < 4
         beside = jnp.where(low, doubled[:, 16:24], doubled[:, 24:32])
         return twice(jnp.concatenate([doubled[:, :16], beside], 1))
 
@@ -508,30 +550,33 @@
 def gathered_cycle(nx, ny, conc_old, chem_old):
     size = conc_old.shape[0]
     half = size // 2
-    copies = 18 + nx * ny - 1
+    copies = 10 + 8 + 14 + 2 * (nx * ny - 1)
     scratch = [
+        conc_old.shape,
+        conc_old.shape,
         (2, size, 8, 128),
         (2, 2, HALO, 16, 128),
         (2, size, 8, 128),
         (4, HALO - 1, 8, 128),
         (2, half, 8, 128),
-        (2, half, 8, 128),
+        (2, 2, half // 2, 8, 128),
         (2, 2, HALO, 8, 128),
-        (2, half, 8, 128),
-        (4, HALO - 1, 8, 128),
+        (2, 2, half // 2, 8, 128),
+        (2, 4, HALO, 8, 128),
         (2, 8, 128),
-        (nx, ny, 2, 8, 128),
-        (half + 2, 32, 128),
+        (2, nx, ny * 8, 128),
+        (2 * nx + half, 8 * ny, 128),
     ]
     shape = jax.ShapeDtypeStruct(conc_old.shape, jnp.float32)
     space = pl.BlockSpec(memory_space=pltpu.VMEM)
+    away = pl.BlockSpec(memory_space=pl.ANY)
     return pl.pallas_call(
         functools.partial(cycle_kernel, nx, ny),
         out_shape=(shape, shape),
-        in_specs=[space, space],
+        in_specs=[away, away],
         out_specs=(space, space),
         scratch_shapes=[pltpu.VMEM(dims, jnp.float32) for dims in scratch]
-        + [pltpu.SemaphoreType.DMA((copies,)), pltpu.SemaphoreType.DMA((copies,))],
+        + [pltpu.SemaphoreType.DMA((count,)) for count in (2, copies, copies)],
         compiler_params=pltpu.CompilerParams(
             collective_id=0, has_side_effects=True, vmem_limit_bytes=32 * 1024 * 1024
         ),
@@ -540,7 +585,7 @@
 
 def body(conc_old, chem_old):
     nx, ny = lax.axis_size("gx"), lax.axis_size("gy")
-    if conc_old.shape == (16, 16, 128) and min(nx, ny) >= 3 and nx * ny <= 16:
+    if conc_old.shape == (16, 16, 128) and nx >= 3 and ny == 4 and nx * ny <= 16:
         return gathered_cycle(nx, ny, conc_old, chem_old)
     result = plain_solve(jnp.stack([conc_old, chem_old]))
     return (result[0], result[1])

time: 34.1 us -> 31.7 us (0.930)
  Pallas kernels: 30.2 us -> 27.8 us
    pallas_call x1, Pallas kernels: 30.2 us -> 27.8 us  [gathered_cycle(): pl.pallas_call(functools.partial(cycle_kernel, nx, ny), out_shape=(shape,...]
where the time goes in v2:
time: 31.7 us; the launch traced here: 31.6 us
  Pallas kernels  27.8 us (88%)
  local copies, waits for them, and re-layouts  3.11 us (10%)
  between operations  0.65 us (2%)
    pallas_call x1, Pallas kernels, gathered_cycle(): pl.pallas_call(functools.partial(cycle_kernel, nx, ny), out_shape=(shape,...  27.8 us
    unnamed x6, local copies, waits for them, and re-layouts  3.11 us

profile of v2, /device:TPU:0, one launch (start us, length us, event | category | flops | bytes accessed | tf_op | source)
XLA Modules:
  0.0 31.6 jit_solution(9508255886560717592)
XLA Ops:
  0.6 0.0 copy-start
  0.6 0.9 %copy-done = f32[16,16,128]{2,1,0:T(8,128)S(1)} copy-done((f32[16,16,128]{2,1,0:T(8,128)S(1)}, f32[16,16,128]{2,1,0:T(8,128)}, u32[]{:S(2)}) %copy-start) | copy-done | bytes 131096
  1.5 0.0 copy-start.1
  1.5 0.9 %copy-done.1 = f32[16,16,128]{2,1,0:T(8,128)S(1)} copy-done((f32[16,16,128]{2,1,0:T(8,128)S(1)}, f32[16,16,128]{2,1,0:T(8,128)}, u32[]{:S(2)}) %copy-start.1) | copy-done | bytes 131096
  2.4 27.8 %shard_map.41 = (f32[16,16,128]{2,1,0:T(8,128)S(1)}, f32[16,16,128]{2,1,0:T(8,128)S(1)}) custom-call(f32[16,16,128]{2,1,0:T(8,128)S(1)} %copy-done, f32[16,16,128]{2,1,0:T(8,128)S(1)} %copy-done.1), custom_call_target="tpu_custom_call" | custom-call | tf_op jit(solution)/shard_map/pallas_call | solution.py:573
  30.2 0.7 %copy.6 = f32[16,16,128]{2,1,0:T(8,128)} copy(f32[16,16,128]{2,1,0:T(8,128)S(1)} %get-tuple-element.4) | data formatting | bytes 262144
  30.9 0.7 %copy.7 = f32[16,16,128]{2,1,0:T(8,128)} copy(f32[16,16,128]{2,1,0:T(8,128)S(1)} %get-tuple-element.5) | data formatting | bytes 262144
Async XLA Ops:
  0.6 0.9 %copy-start = (f32[16,16,128]{2,1,0:T(8,128)S(1)}, f32[16,16,128]{2,1,0:T(8,128)}, u32[]{:S(2)}) copy-start(f32[16,16,128]{2,1,0:T(8,128)} %conc_ref.1) | copy-start | bytes 393220
  1.5 0.9 %copy-start.1 = (f32[16,16,128]{2,1,0:T(8,128)S(1)}, f32[16,16,128]{2,1,0:T(8,128)}, u32[]{:S(2)}) copy-start(f32[16,16,128]{2,1,0:T(8,128)} %chem_ref.1) | copy-start | bytes 393220

commit v3 on v2

--- a/solution.py
+++ b/solution.py
@@ -219,53 +219,78 @@
     return jnp.concatenate([values[i // 2 : i // 2 + 1] for i in range(2 * values.shape[0])], 0)
 
 
+class Strip:
+    def __init__(self, start, cells):
+        self.start, self.cells = start, cells
+
+    def at(self, low, high):
+        return self.cells[low - self.start : high - self.start]
+
+
+def strips(*parts):
+    return Strip(parts[0].start, jnp.concatenate([part.cells for part in parts], 0))
+
+
 class Level:
-    def __init__(self, scale, mob, mob_sum, row_step, lane_step, wrap=False):
-        self.scale, self.mob = scale, mob
+    def __init__(self, scale, row_step, lane_step, wrap=False):
+        self.scale = scale
         self.row_step, self.lane_step, self.wrap = row_step, lane_step, wrap
         self.half = 0.5 * TIME_STEP * scale
         self.diagonal = STABILIZER + 6.0 * GRADIENT_ENERGY * scale
-        self.coupling = self.half * (6.0 * mob + mob_sum)
-        self.damp = DAMPING / (1.0 + self.coupling * self.diagonal)
-
-    def part(self, values, size):
-        off = (values.shape[0] - size) // 2
-        return values[off : off + size]
-
-    def residual(self, conc, chem, right):
-        size = conc.shape[0] if self.wrap else conc.shape[0] - 2
-        sums = functools.partial(
-            near_sum, row_step=self.row_step, lane_step=self.lane_step, wrap=self.wrap
-        )
-        carried = self.part(self.mob, conc.shape[0]) * chem
-        mob = self.part(self.mob, size)
-        c, u = self.part(conc, size), self.part(chem, size)
+        self.mob = self.coupling = self.damp = None
+
+    def set(self, mob, coupling):
+        self.mob = mob
+        self.coupling = coupling
+        self.damp = Strip(coupling.start, DAMPING / (1.0 + coupling.cells * self.diagonal))
+        return self
+
+    def sums(self, values):
+        return near_sum(values, self.row_step, self.lane_step, self.wrap)
+
+    def coupled(self, mob, mob_sum):
+        return self.half * (6.0 * mob + mob_sum)
+
+    def residual(self, conc, chem, right, low, high):
+        rim = 0 if self.wrap else 1
+        c, u, mob = conc.at(low, high), chem.at(low, high), self.mob.at(low, high)
+        near_chem = chem.at(low - rim, high + rim)
+        carried = self.mob.at(low - rim, high + rim) * near_chem
         first = (
-            self.part(right[0], size)
+            right[0].at(low, high)
             - c
-            + self.half * (mob * sums(chem) + sums(carried))
-            - self.part(self.coupling, size) * u
-        )
-        near = sums(conc) - 6.0 * c
+            + self.half * (mob * self.sums(near_chem) + self.sums(carried))
+            - self.coupling.at(low, high) * u
+        )
+        near = self.sums(conc.at(low - rim, high + rim)) - 6.0 * c
         second = (
-            self.part(right[1], size)
+            right[1].at(low, high)
             - u
             + STABILIZER * c
             - (GRADIENT_ENERGY * self.scale) * near
         )
         return first, second
 
-    def step(self, first, second):
-        size = first.shape[0]
-        damp = self.part(self.damp, size)
-        coupling = self.part(self.coupling, size)
-        return damp * (first - coupling * second), damp * (second + self.diagonal * first)
-
-    def sweep(self, conc, chem, right):
-        first, second = self.residual(conc, chem, right)
-        size = first.shape[0]
-        dc, du = self.step(first, second)
-        return self.part(conc, size) + dc, self.part(chem, size) + du
+    def step(self, first, second, low):
+        high = low + first.shape[0]
+        damp = self.damp.at(low, high)
+        coupling = self.coupling.at(low, high)
+        conc_step = damp * (first - coupling * second)
+        return Strip(low, conc_step), Strip(low, damp * (second + self.diagonal * first))
+
+    def sweep(self, conc, chem, right, low, high):
+        dc, du = self.step(*self.residual(conc, chem, right, low, high), low)
+        return Strip(low, conc.at(low, high) + dc.cells), Strip(low, chem.at(low, high) + du.cells)
+
+    def sweeps(self, count, conc, chem, right):
+        size = conc.cells.shape[0]
+
+        def once(_, now):
+            new = self.sweep(Strip(0, now[0]), Strip(0, now[1]), right, 0, size)
+            return new[0].cells, new[1].cells
+
+        now = lax.fori_loop(0, count, once, (conc.cells, chem.cells))
+        return Strip(0, now[0]), Strip(0, now[1])
 
 
 def split_halves(first, second, first_high, second_high):
@@ -343,17 +368,16 @@
     edge0[1] = split_halves(conc[:, -8:], chem[:, -8:], True, True)
     pl.semaphore_wait(barrier, len(peers))
 
-    waits = []
+    outer, beside = [], []
     for side, dx in ((0, -1), (1, 1)):
         rows = pl.ds(0, HALO) if dx < 0 else pl.ds(size - HALO, HALO)
-        waits.append(send(own_conc.at[rows], from_x0.at[side, 0], dx, 0))
-        waits.append(send(own_chem.at[rows], from_x0.at[side, 1], dx, 0))
+        outer.append(send(own_conc.at[rows], from_x0.at[side, 0], dx, 0))
+        outer.append(send(own_chem.at[rows], from_x0.at[side, 1], dx, 0))
+    for side, dy in ((0, -1), (1, 1)):
+        beside.append(send(edge0.at[side], from_y0.at[side], 0, dy))
     for place, (dx, dy) in enumerate(CORNERS):
         rows = pl.ds(0, HALO - 1) if dx < 0 else pl.ds(size - HALO + 1, HALO - 1)
-        waits.append(send(edge0.at[(dy + 1) // 2, rows], from_d0.at[place], dx, dy))
-    for side, dy in ((0, -1), (1, 1)):
-        waits.append(send(edge0.at[side], from_y0.at[side], 0, dy))
-    arrive(waits)
+        outer.append(send(edge0.at[(dy + 1) // 2, rows], from_d0.at[place], dx, dy))
 
     def halo_rows(center, lower, upper):
         return jnp.concatenate([lower[:1], lower, center, upper, upper[-1:]], 0)
@@ -361,14 +385,6 @@
     def joined(right, left):
         low = iota(right.shape, 1) < 4
         return jnp.where(low, right, turn(left, 4, 1)), jnp.where(low, turn(right, 4, 1), left)
-
-    right0 = halo_rows(from_y0[0], from_d0[2], from_d0[0])
-    left0 = halo_rows(from_y0[1], from_d0[3], from_d0[1])
-    conc_halo, chem_halo = joined(right0, left0)
-    conc = jnp.concatenate([from_x0[1, 0], conc, from_x0[0, 0]], 0)
-    chem = jnp.concatenate([from_x0[1, 1], chem, from_x0[0, 1]], 0)
-    conc = jnp.concatenate([conc, conc_halo], 1)
-    chem = jnp.concatenate([chem, chem_halo], 1)
 
     def row_pairs(values):
         count, rows = values.shape[:2]
@@ -453,8 +469,42 @@
             [jnp.concatenate(inside, 0), halo_rows(center, lower, upper)], 1
         )
 
-    mob0 = mobility_of(conc)
-    mob_x = pair_sum(pair_rows(mob0[2:-2]), 1, 2) * 0.125
+    def fields_of(start, inside, right, left):
+        halos = joined(right, left)
+        return tuple(
+            Strip(start, jnp.concatenate([cells, halo], 1)) for cells, halo in zip(inside, halos)
+        )
+
+    def right_of_strip(conc):
+        cells = conc.cells
+        return conc, Strip(conc.start, cells * cells * cells - (1.0 + STABILIZER) * cells)
+
+    arrive(beside)
+    level0 = Level(1.0, 1, 1)
+    middle = fields_of(0, (conc, chem), from_y0[0], from_y0[1])
+    mob_middle = Strip(0, mobility_of(middle[0].cells))
+    coupling = Strip(1, level0.coupled(mob_middle.at(1, size - 1), level0.sums(mob_middle.cells)))
+    level0.set(mob_middle, coupling)
+    damp_middle = level0.damp
+    right_middle = right_of_strip(middle[0])
+    once_middle = level0.sweep(*middle, right_middle, 1, size - 1)
+    both_middle = level0.sweep(*once_middle, right_middle, 2, size - 2)
+    defect_middle = level0.residual(*both_middle, right_middle, 3, size - 3)
+
+    arrive(outer)
+    low_right = jnp.concatenate([from_d0[2][:1], from_d0[2]], 0)
+    low_left = jnp.concatenate([from_d0[3][:1], from_d0[3]], 0)
+    high_right = jnp.concatenate([from_d0[0], from_d0[0][-1:]], 0)
+    high_left = jnp.concatenate([from_d0[1], from_d0[1][-1:]], 0)
+    lows = fields_of(-HALO, (from_x0[1, 0], from_x0[1, 1]), low_right, low_left)
+    highs = fields_of(size, (from_x0[0, 0], from_x0[0, 1]), high_right, high_left)
+    fields = tuple(strips(*parts) for parts in zip(lows, middle, highs))
+    mob_low, mob_high = (Strip(part[0].start, mobility_of(part[0].cells)) for part in (lows, highs))
+    mob0 = strips(mob_low, mob_middle, mob_high)
+    right_low, right_high = right_of_strip(lows[0]), right_of_strip(highs[0])
+    right_side0 = tuple(strips(*parts) for parts in zip(right_low, right_middle, right_high))
+
+    mob_x = pair_sum(pair_rows(mob0.at(-2, size + 2)), 1, 2) * 0.125
     mob1 = row_pairs(jnp.concatenate([mob_x, mob_x[:, 16:24]], 1))
     mob1_sum = near_sum(mob1, 1, 2)[:, :8]
     mob1 = mob1[1:-1, :8]
@@ -464,36 +514,54 @@
     pack2[1] = by_lane(twice_pair(pair_sum(pair_rows(mob1), 2, 2) * 0.125))
     mob2_waits = gather(1)
 
-    level0 = Level(1.0, mob0[1:-1], near_sum(mob0, 1, 1), 1, 1)
-    level0.mob = mob0
-    right_side0 = (conc, conc * conc * conc - (1.0 + STABILIZER) * conc)
-    conc, chem = level0.sweep(conc, chem, right_side0)
-    conc, chem = level0.sweep(conc, chem, right_side0)
-    fields0 = (conc, chem)
-    first, second = level0.residual(
-        level0.part(conc, size + 2), level0.part(chem, size + 2), right_side0
-    )
-    whole1[0] = jnp.where(even1, coarse(first[:, :16], 1), coarse(second[:, :16], 1))
+    def outer_coupling(low, high):
+        near = level0.sums(mob0.at(low - 1, high + 1))
+        return Strip(low, level0.coupled(mob0.at(low, high), near))
+
+    coupling_low, coupling_high = outer_coupling(-3, 1), outer_coupling(size - 1, size + 3)
+    level0.set(mob0, coupling_low)
+    damp_low = level0.damp
+    level0.set(mob0, coupling_high)
+    level0.damp = strips(damp_low, damp_middle, level0.damp)
+    level0.coupling = strips(coupling_low, coupling, coupling_high)
+
+    def completed(now, before, low, high):
+        inner = now[0].start, now[0].start + now[0].cells.shape[0]
+        below = level0.sweep(*before, right_side0, low, inner[0])
+        above = level0.sweep(*before, right_side0, inner[1], high)
+        return tuple(strips(*parts) for parts in zip(below, now, above))
+
+    once = completed(once_middle, fields, -3, size + 3)
+    fields0 = completed(both_middle, once, -2, size + 2)
+    below = level0.residual(*fields0, right_side0, 0, 3)
+    above = level0.residual(*fields0, right_side0, size - 3, size)
+    first, second = (
+        jnp.concatenate(parts, 0)[:, :16] for parts in zip(below, defect_middle, above)
+    )
+    whole1[0] = jnp.where(even1, coarse(first, 1), coarse(second, 1))
     near_waits, far_waits = swap1(0, 2)
 
     arrive(mob1_waits)
     mob1, mob1_sum = spread(padded1(1, HALO), 1, 2)
-    level1 = Level(0.25, mob1, mob1_sum, 1, 2)
+    level1 = Level(0.25, 1, 2)
+    level1.set(Strip(-HALO, mob1), Strip(-HALO, level1.coupled(mob1, mob1_sum)))
     arrive(near_waits)
     rhs1 = spread(padded1(0, 2), 1, 2)
-    conc, chem = level1.step(*rhs1)
-    conc, chem = level1.sweep(conc, chem, rhs1)
+    conc, chem = level1.step(*rhs1, -2)
+    rhs1 = [Strip(-2, values) for values in rhs1]
+    conc, chem = level1.sweep(conc, chem, rhs1, -1, half + 1)
     own = [
         twice_pair(pair_sum(pair_rows(values[:, :8]), 2, 2) * 0.125)
-        for values in level1.residual(conc, chem, rhs1)
+        for values in level1.residual(conc, chem, rhs1, 0, half)
     ]
     pack2[0] = jnp.where(iota((8, 128), 0) % 2 == 0, by_lane(own[0]), by_lane(own[1]))
     rhs2_waits = gather(0)
 
     arrive(far_waits)
     rhs1 = spread(padded1(0, HALO), 1, 2)
-    conc, chem = level1.step(*rhs1)
-    fields1 = level1.sweep(conc, chem, rhs1)
+    conc, chem = level1.step(*rhs1, -HALO)
+    rhs1 = [Strip(-HALO, values) for values in rhs1]
+    fields1 = level1.sweep(conc, chem, rhs1, -3, half + 3)
 
     def by_row(values):
         zero, one = spread(values, 1, 2)
@@ -504,22 +572,23 @@
 
     arrive(mob2_waits)
     mob2 = by_row(grid2[1, :, pl.ds(0, 4 * ny, stride=2)])
-    level2 = Level(0.0625, mob2, near_sum(mob2, 1, 4, True), 1, 4, True)
     mob3 = coarse(mob2, 4)
-    level3 = Level(0.015625, mob3, near_sum(mob3, 1, 8, True), 1, 8, True)
+    level2, level3 = Level(0.0625, 1, 4, True), Level(0.015625, 1, 8, True)
+    for level, mob in ((level2, mob2), (level3, mob3)):
+        level.set(Strip(0, mob), Strip(0, level.coupled(mob, level.sums(mob))))
 
     arrive(rhs2_waits)
     rhs2 = [by_row(grid2[0, :, pl.ds(start, 4 * ny, stride=2)]) for start in (0, 1)]
-    conc, chem = level2.step(*rhs2)
-    conc, chem = level2.sweep(conc, chem, rhs2)
-    rhs3 = [coarse(v, 4) for v in level2.residual(conc, chem, rhs2)]
-    low_conc, low_chem = level3.step(*rhs3)
-    for _ in range(COARSE - 1):
-        low_conc, low_chem = level3.sweep(low_conc, low_chem, rhs3)
-    conc = conc + twice(rows_twice(low_conc))
-    chem = chem + twice(rows_twice(low_chem))
-    for _ in range(SWEEPS):
-        conc, chem = level2.sweep(conc, chem, rhs2)
+    conc, chem = level2.step(*rhs2, 0)
+    rhs2 = [Strip(0, values) for values in rhs2]
+    conc, chem = level2.sweep(conc, chem, rhs2, 0, nx * quarter)
+    rhs3 = [coarse(v, 4) for v in level2.residual(conc, chem, rhs2, 0, nx * quarter)]
+    low_conc, low_chem = level3.step(*rhs3, 0)
+    rhs3 = [Strip(0, values) for values in rhs3]
+    low_conc, low_chem = level3.sweeps(COARSE - 1, low_conc, low_chem, rhs3)
+    conc = Strip(0, conc.cells + twice(rows_twice(low_conc.cells)))
+    chem = Strip(0, chem.cells + twice(rows_twice(low_chem.cells)))
+    conc, chem = level2.sweeps(SWEEPS, conc, chem, rhs2)
 
     def around1(values):
         values = jnp.concatenate([values[-2:], values[: quarter + 2]], 0)
@@ -528,9 +597,11 @@
         beside = jnp.where(low, values[:, 8:16], values[:, -8:])
         return twice(jnp.concatenate([values[:, :8], beside], 1))[1:-1]
 
-    conc, chem = fields1[0] + around1(conc), fields1[1] + around1(chem)
-    for _ in range(SWEEPS):
-        conc, chem = level1.sweep(conc, chem, rhs1)
+    conc, chem = (
+        Strip(-3, old.cells + around1(new.cells)) for old, new in zip(fields1, (conc, chem))
+    )
+    conc, chem = level1.sweep(conc, chem, rhs1, -2, half + 2)
+    conc, chem = level1.sweep(conc, chem, rhs1, -1, half + 1)
 
     def around0(values):
         doubled = rows_twice(values)
@@ -538,11 +609,13 @@
         beside = jnp.where(low, doubled[:, 16:24], doubled[:, 24:32])
         return twice(jnp.concatenate([doubled[:, :16], beside], 1))
 
-    conc, chem = fields0[0] + around0(conc), fields0[1] + around0(chem)
-    for _ in range(SWEEPS):
-        conc, chem = level0.sweep(conc, chem, right_side0)
-    conc_out[...] = conc[:, :16]
-    chem_out[...] = chem[:, :16]
+    conc, chem = (
+        Strip(-2, old.cells + around0(new.cells)) for old, new in zip(fields0, (conc, chem))
+    )
+    conc, chem = level0.sweep(conc, chem, right_side0, -1, size + 1)
+    conc, chem = level0.sweep(conc, chem, right_side0, 0, size)
+    conc_out[...] = conc.cells[:, :16]
+    chem_out[...] = chem.cells[:, :16]
     for copy in started:
         copy.wait_send()
 
@@ -578,7 +651,7 @@
         scratch_shapes=[pltpu.VMEM(dims, jnp.float32) for dims in scratch]
         + [pltpu.SemaphoreType.DMA((count,)) for count in (2, copies, copies)],
         compiler_params=pltpu.CompilerParams(
-            collective_id=0, has_side_effects=True, vmem_limit_bytes=32 * 1024 * 1024
+            collective_id=0, has_side_effects=True, vmem_limit_bytes=60 * 1024 * 1024
         ),
     )(conc_old, chem_old)
 

time: 31.7 us -> 31.7 us (level)
  Pallas kernels: 27.8 us -> 28.7 us
  local copies, waits for them, and re-layouts: 3.11 us -> 2.26 us
    pallas_call x1, Pallas kernels: 27.8 us -> 28.7 us  [gathered_cycle(): pl.pallas_call(functools.partial(cycle_kernel, nx, ny), out_shape=(shape,...]
    unnamed x6 -> x4, local copies, waits for them, and re-layouts: 3.11 us -> 2.26 us
where the time goes in v3:
time: 31.7 us; the launch traced here: 31.6 us
  Pallas kernels  28.7 us (91%)
  local copies, waits for them, and re-layouts  2.26 us (7%)
  between operations  0.65 us (2%)
    pallas_call x1, Pallas kernels, gathered_cycle(): pl.pallas_call(functools.partial(cycle_kernel, nx, ny), out_shape=(shape,...  28.7 us
    unnamed x4, local copies, waits for them, and re-layouts  2.26 us

profile of v3, /device:TPU:0, one launch (start us, length us, event | category | flops | bytes accessed | tf_op | source)
XLA Modules:
  0.0 31.6 jit_solution(16032853207851481511)
XLA Ops:
  0.6 28.7 %shard_map.41 = (f32[16,16,128]{2,1,0:T(8,128)}, f32[16,16,128]{2,1,0:T(8,128)}) custom-call(f32[16,16,128]{2,1,0:T(8,128)} %conc_ref.1, f32[16,16,128]{2,1,0:T(8,128)} %chem_ref.1), custom_call_target="tpu_custom_call" | custom-call | tf_op jit(solution)/shard_map/pallas_call | solution.py:646
  29.3 0.0 copy-start
  29.3 1.6 %copy.6 = f32[16,16,128]{2,1,0:T(8,128)} copy(f32[16,16,128]{2,1,0:T(8,128)} %get-tuple-element.4) | data formatting | bytes 262144
  30.9 0.0 copy-done
  30.9 0.7 %copy.7 = f32[16,16,128]{2,1,0:T(8,128)} copy(f32[16,16,128]{2,1,0:T(8,128)S(1)} %copy-done) | data formatting | bytes 262144
Async XLA Ops:
  29.3 1.6 %copy-start = (f32[16,16,128]{2,1,0:T(8,128)S(1)}, f32[16,16,128]{2,1,0:T(8,128)}, u32[]{:S(2)}) copy-start(f32[16,16,128]{2,1,0:T(8,128)} %get-tuple-element.5) | copy-start | bytes 393220

commit v4 on v3

--- a/solution.py
+++ b/solution.py
@@ -300,10 +300,8 @@
     return jnp.where(low, first, second)
 
 
-def cycle_kernel(nx, ny, conc_ref, chem_ref, conc_out, chem_out, *scratch):
+def cycle_kernel(nx, ny, own, result, *scratch):
     (
-        own_conc,
-        own_chem,
         edge0,
         from_x0,
         from_y0,
@@ -316,28 +314,23 @@
         pack2,
         grid2,
         rows_buf,
-        load_sem,
         send_sem,
         recv_sem,
+        spread_sem,
     ) = scratch
     img, gx, gy = lax.axis_index("img"), lax.axis_index("gx"), lax.axis_index("gy")
-    loads = [
-        pltpu.make_async_copy(conc_ref, own_conc, load_sem.at[0]),
-        pltpu.make_async_copy(chem_ref, own_chem, load_sem.at[1]),
-    ]
-    for load in loads:
-        load.start()
+    x_at = [lax.rem(gx + dx, nx) for dx in range(nx)]
+    y_at = [lax.rem(gy + dy, ny) for dy in range(ny)]
 
     def at(dx, dy):
-        return (img, lax.rem(gx + dx + nx, nx), lax.rem(gy + dy + ny, ny))
-
-    peers = [(dx, dy) for dx in range(nx) for dy in range(ny) if (dx, dy) != (0, 0)]
+        return (img, x_at[dx % nx], y_at[dy % ny])
+
+    peers = [(dx, dy) for dx in [*range(1, nx), 0] for dy in range(ny) if (dx, dy) != (0, 0)]
     barrier = pltpu.get_barrier_semaphore()
     for dx, dy in peers:
         pl.semaphore_signal(barrier, inc=1, device_id=at(dx, dy), device_id_type=MESH)
 
     used = [0]
-    started = []
 
     def send(src, dst, dx, dy):
         index = used[0]
@@ -351,19 +344,16 @@
             device_id_type=MESH,
         )
         copy.start()
-        started.append(copy)
         return copy
 
     def arrive(copies):
         for copy in copies:
             copy.wait_recv()
 
-    for load in loads:
-        load.wait()
-    size = own_conc.shape[0]
+    size = own.shape[1]
     half = size // 2
     quarter = half // 2
-    conc, chem = own_conc[...], own_chem[...]
+    conc, chem = own[0], own[1]
     edge0[0] = split_halves(conc[:, :8], chem[:, :8], False, False)
     edge0[1] = split_halves(conc[:, -8:], chem[:, -8:], True, True)
     pl.semaphore_wait(barrier, len(peers))
@@ -371,8 +361,7 @@
     outer, beside = [], []
     for side, dx in ((0, -1), (1, 1)):
         rows = pl.ds(0, HALO) if dx < 0 else pl.ds(size - HALO, HALO)
-        outer.append(send(own_conc.at[rows], from_x0.at[side, 0], dx, 0))
-        outer.append(send(own_chem.at[rows], from_x0.at[side, 1], dx, 0))
+        outer.append(send(own.at[:, rows], from_x0.at[side], dx, 0))
     for side, dy in ((0, -1), (1, 1)):
         beside.append(send(edge0.at[side], from_y0.at[side], 0, dy))
     for place, (dx, dy) in enumerate(CORNERS):
@@ -422,12 +411,34 @@
         return pair_sum(values, 1, 1)
 
     def gather(kind):
-        copies = []
         for dx, dy in peers:
             rows = pl.ds(8 * ((ny - dy) % ny), 8)
-            copies.append(send(pack2.at[kind], grid2.at[kind, (nx - dx) % nx, rows], dx, dy))
+            index = 2 * kind + (dx == 0)
+            pltpu.make_async_remote_copy(
+                src_ref=pack2.at[kind],
+                dst_ref=grid2.at[kind, (nx - dx) % nx, rows],
+                send_sem=spread_sem.at[0, index],
+                recv_sem=spread_sem.at[1, index],
+                device_id=at(dx, dy),
+                device_id_type=MESH,
+            ).start()
         grid2[kind, 0, :8] = pack2[kind]
-        return copies
+        views = grid2.at[kind, pl.ds(1, nx - 1)], grid2.at[kind, 0, pl.ds(8, 8 * ny - 8)]
+        return [
+            pltpu.make_async_remote_copy(
+                src_ref=view,
+                dst_ref=view,
+                send_sem=spread_sem.at[0, 2 * kind + index],
+                recv_sem=spread_sem.at[1, 2 * kind + index],
+                device_id=at(1 - index, index),
+                device_id_type=MESH,
+            )
+            for index, view in enumerate(views)
+        ]
+
+    def drain(copies):
+        for copy in copies:
+            copy.wait_send()
 
     def swap1(kind, inner):
         first, rest = [], []
@@ -479,6 +490,10 @@
         cells = conc.cells
         return conc, Strip(conc.start, cells * cells * cells - (1.0 + STABILIZER) * cells)
 
+    mob1 = coarse(mobility_of(conc), 1)
+    pack2[1] = by_lane(twice_pair(pair_sum(pair_rows(mob1), 2, 2) * 0.125))
+    mob2_waits = gather(1)
+
     arrive(beside)
     level0 = Level(1.0, 1, 1)
     middle = fields_of(0, (conc, chem), from_y0[0], from_y0[1])
@@ -511,8 +526,6 @@
     even1 = iota((half, 8, 128), 2) % 2 == 0
     whole1[1] = jnp.where(even1, mob1, mob1_sum)
     mob1_waits, _ = swap1(1, HALO)
-    pack2[1] = by_lane(twice_pair(pair_sum(pair_rows(mob1), 2, 2) * 0.125))
-    mob2_waits = gather(1)
 
     def outer_coupling(low, high):
         near = level0.sums(mob0.at(low - 1, high + 1))
@@ -545,6 +558,22 @@
     mob1, mob1_sum = spread(padded1(1, HALO), 1, 2)
     level1 = Level(0.25, 1, 2)
     level1.set(Strip(-HALO, mob1), Strip(-HALO, level1.coupled(mob1, mob1_sum)))
+    drain(outer + beside + mob1_waits)
+    def by_row(values):
+        zero, one = spread(values, 1, 2)
+        zero, two = spread(zero, 2, 2)
+        one, three = spread(one, 2, 2)
+        together = jnp.stack([zero, one, two, three], 1)
+        return together.reshape((nx * quarter,) + values.shape[1:])
+
+    arrive(mob2_waits)
+    mob2 = by_row(grid2[1, :, pl.ds(0, 4 * ny, stride=2)])
+    mob3 = coarse(mob2, 4)
+    level2, level3 = Level(0.0625, 1, 4, True), Level(0.015625, 1, 8, True)
+    for level, mob in ((level2, mob2), (level3, mob3)):
+        level.set(Strip(0, mob), Strip(0, level.coupled(mob, level.sums(mob))))
+
+    drain(mob2_waits)
     arrive(near_waits)
     rhs1 = spread(padded1(0, 2), 1, 2)
     conc, chem = level1.step(*rhs1, -2)
@@ -563,20 +592,7 @@
     rhs1 = [Strip(-HALO, values) for values in rhs1]
     fields1 = level1.sweep(conc, chem, rhs1, -3, half + 3)
 
-    def by_row(values):
-        zero, one = spread(values, 1, 2)
-        zero, two = spread(zero, 2, 2)
-        one, three = spread(one, 2, 2)
-        together = jnp.stack([zero, one, two, three], 1)
-        return together.reshape((nx * quarter,) + values.shape[1:])
-
-    arrive(mob2_waits)
-    mob2 = by_row(grid2[1, :, pl.ds(0, 4 * ny, stride=2)])
-    mob3 = coarse(mob2, 4)
-    level2, level3 = Level(0.0625, 1, 4, True), Level(0.015625, 1, 8, True)
-    for level, mob in ((level2, mob2), (level3, mob3)):
-        level.set(Strip(0, mob), Strip(0, level.coupled(mob, level.sums(mob))))
-
+    drain(near_waits + far_waits)
     arrive(rhs2_waits)
     rhs2 = [by_row(grid2[0, :, pl.ds(start, 4 * ny, stride=2)]) for start in (0, 1)]
     conc, chem = level2.step(*rhs2, 0)
@@ -614,19 +630,16 @@
     )
     conc, chem = level0.sweep(conc, chem, right_side0, -1, size + 1)
     conc, chem = level0.sweep(conc, chem, right_side0, 0, size)
-    conc_out[...] = conc.cells[:, :16]
-    chem_out[...] = chem.cells[:, :16]
-    for copy in started:
-        copy.wait_send()
-
-
-def gathered_cycle(nx, ny, conc_old, chem_old):
-    size = conc_old.shape[0]
+    result[0] = conc.cells[:, :16]
+    result[1] = chem.cells[:, :16]
+    drain(rhs2_waits)
+
+
+def gathered_cycle(nx, ny, fields):
+    size = fields.shape[1]
     half = size // 2
-    copies = 10 + 8 + 14 + 2 * (nx * ny - 1)
+    copies = 8 + 8 + 14
     scratch = [
-        conc_old.shape,
-        conc_old.shape,
         (2, size, 8, 128),
         (2, 2, HALO, 16, 128),
         (2, size, 8, 128),
@@ -640,27 +653,28 @@
         (2, nx, ny * 8, 128),
         (2 * nx + half, 8 * ny, 128),
     ]
-    shape = jax.ShapeDtypeStruct(conc_old.shape, jnp.float32)
+    shape = jax.ShapeDtypeStruct(fields.shape, jnp.float32)
     space = pl.BlockSpec(memory_space=pltpu.VMEM)
-    away = pl.BlockSpec(memory_space=pl.ANY)
     return pl.pallas_call(
         functools.partial(cycle_kernel, nx, ny),
-        out_shape=(shape, shape),
-        in_specs=[away, away],
-        out_specs=(space, space),
+        out_shape=shape,
+        in_specs=[space],
+        out_specs=space,
         scratch_shapes=[pltpu.VMEM(dims, jnp.float32) for dims in scratch]
-        + [pltpu.SemaphoreType.DMA((count,)) for count in (2, copies, copies)],
+        + [pltpu.SemaphoreType.DMA((count,)) for count in (copies, copies)]
+        + [pltpu.SemaphoreType.DMA((2, 4))],
         compiler_params=pltpu.CompilerParams(
-            collective_id=0, has_side_effects=True, vmem_limit_bytes=60 * 1024 * 1024
+            collective_id=0, has_side_effects=True, vmem_limit_bytes=32 * 1024 * 1024
         ),
-    )(conc_old, chem_old)
+    )(fields)
 
 
 def body(conc_old, chem_old):
     nx, ny = lax.axis_size("gx"), lax.axis_size("gy")
     if conc_old.shape == (16, 16, 128) and nx >= 3 and ny == 4 and nx * ny <= 16:
-        return gathered_cycle(nx, ny, conc_old, chem_old)
-    result = plain_solve(jnp.stack([conc_old, chem_old]))
+        result = gathered_cycle(nx, ny, jnp.stack([conc_old, chem_old]))
+    else:
+        result = plain_solve(jnp.stack([conc_old, chem_old]))
     return (result[0], result[1])
 
 

time: 31.7 us -> 29.3 us (0.924)
  Pallas kernels: 28.7 us -> 26.8 us
  local copies, waits for them, and re-layouts: 2.26 us -> 0.72 us
  other arithmetic: 0 us -> 0.99 us
    unnamed x4 -> x0, local copies, waits for them, and re-layouts: 2.26 us -> none
    pallas_call x1, Pallas kernels: 28.7 us -> 26.8 us  [gathered_cycle(): pl.pallas_call(functools.partial(cycle_kernel, nx, ny), out_shape=shape,...]
    another operation x0 -> x1, other arithmetic: none -> 0.99 us  [body(): result = gathered_cycle(nx, ny, jnp.stack([conc_old, chem_old]))]
    squeeze x0 -> x1, local copies, waits for them, and re-layouts: none -> 0.72 us  [body(): return (result[0], result[1])]
where the time goes in v4:
time: 29.3 us; the launch traced here: 29.1 us
  Pallas kernels  26.8 us (91%)
  other arithmetic  0.99 us (3%)
  local copies, waits for them, and re-layouts  0.72 us (2%)
  between operations  0.64 us (2%)
    pallas_call x1, Pallas kernels, gathered_cycle(): pl.pallas_call(functools.partial(cycle_kernel, nx, ny), out_shape=shape,...  26.8 us
    another operation x1, other arithmetic, body(): result = gathered_cycle(nx, ny, jnp.stack([conc_old, chem_old]))  0.99 us
    squeeze x1, local copies, waits for them, and re-layouts, body(): return (result[0], result[1])  0.72 us

profile of v4, /device:TPU:0, one launch (start us, length us, event | category | flops | bytes accessed | tf_op | source)
XLA Modules:
  0.0 29.1 jit_solution(10136920996767179798)
XLA Ops:
  0.6 1.0 %pad_maximum_fusion.own = f32[2,16,16,128]{3,2,1,0:T(8,128)S(1)} fusion(f32[1,16,16,128]{3,2,1,0:T(8,128)} %bitcast.6, f32[1,16,16,128]{3,2,1,0:T(8,128)} %bitcast.7), kind=kLoop, calls=%fused_computation | loop fusion | flops 65536 | bytes 524288 | tf_op jit(solution)/shard_map/stack | solution.py:675
  1.6 26.8 %shard_map.41 = f32[2,16,16,128]{3,2,1,0:T(8,128)S(1)} custom-call(f32[2,16,16,128]{3,2,1,0:T(8,128)S(1)} %pad_maximum_fusion.own), custom_call_target="tpu_custom_call" | custom-call | tf_op jit(solution)/shard_map/pallas_call | solution.py:658
  28.4 0.7 %slice_bitcast_fusion = (f32[16,16,128]{2,1,0:T(8,128)}, f32[16,16,128]{2,1,0:T(8,128)}) fusion(f32[2,16,16,128]{3,2,1,0:T(8,128)S(1)} %shard_map.41), kind=kLoop, calls=%fused_computation.1 | loop fusion | bytes 524288 | tf_op jit(solution)/shard_map/squeeze | solution.py:678

commit v5 on v4

--- a/solution.py
+++ b/solution.py
@@ -192,15 +192,9 @@
     return pltpu.roll(values, shift % size, axis)
 
 
-def near_sum(values, row_step, lane_step, wrap=False):
-    if wrap:
-        middle = values
-        total = jnp.concatenate([values[1:], values[:1]], 0) + jnp.concatenate(
-            [values[-1:], values[:-1]], 0
-        )
-    else:
-        middle = values[1:-1]
-        total = values[2:] + values[:-2]
+def near_sum(values, row_step, lane_step):
+    middle = values[1:-1]
+    total = values[2:] + values[:-2]
     total = total + (turn(middle, row_step, 1) + turn(middle, -row_step, 1))
     return total + (turn(middle, lane_step, 2) + turn(middle, -lane_step, 2))
 
@@ -231,38 +225,49 @@
     return Strip(parts[0].start, jnp.concatenate([part.cells for part in parts], 0))
 
 
+def wrapped(strip):
+    cells = strip.cells
+    return Strip(strip.start - 1, jnp.concatenate([cells[-1:], cells, cells[:1]], 0))
+
+
 class Level:
-    def __init__(self, scale, row_step, lane_step, wrap=False):
-        self.scale = scale
+    def __init__(self, scale, row_step, lane_step, layers, wrap=False):
+        self.scale, self.layers = scale, layers
         self.row_step, self.lane_step, self.wrap = row_step, lane_step, wrap
         self.half = 0.5 * TIME_STEP * scale
         self.diagonal = STABILIZER + 6.0 * GRADIENT_ENERGY * scale
         self.mob = self.coupling = self.damp = None
 
-    def set(self, mob, coupling):
+    def pieces(self, work, low, high):
+        parts = [
+            work(at, min(at + self.layers, high)) for at in range(low, high, self.layers)
+        ]
+        return tuple(Strip(low, jnp.concatenate(cells, 0)) for cells in zip(*parts))
+
+    def sums(self, values):
+        return near_sum(values, self.row_step, self.lane_step)
+
+    def setup(self, mob, low, high, mob_sum=None):
+        def work(low, high):
+            near = self.sums(mob.at(low - 1, high + 1)) if mob_sum is None else mob_sum.at(low, high)
+            coupling = self.half * (6.0 * mob.at(low, high) + near)
+            return coupling, DAMPING / (1.0 + coupling * self.diagonal)
+
         self.mob = mob
-        self.coupling = coupling
-        self.damp = Strip(coupling.start, DAMPING / (1.0 + coupling.cells * self.diagonal))
-        return self
-
-    def sums(self, values):
-        return near_sum(values, self.row_step, self.lane_step, self.wrap)
-
-    def coupled(self, mob, mob_sum):
-        return self.half * (6.0 * mob + mob_sum)
-
-    def residual(self, conc, chem, right, low, high):
-        rim = 0 if self.wrap else 1
+        self.coupling, self.damp = self.pieces(work, low, high)
+        return self.coupling, self.damp
+
+    def defect(self, conc, chem, right, low, high):
         c, u, mob = conc.at(low, high), chem.at(low, high), self.mob.at(low, high)
-        near_chem = chem.at(low - rim, high + rim)
-        carried = self.mob.at(low - rim, high + rim) * near_chem
+        near_chem = chem.at(low - 1, high + 1)
+        carried = self.mob.at(low - 1, high + 1) * near_chem
         first = (
             right[0].at(low, high)
             - c
             + self.half * (mob * self.sums(near_chem) + self.sums(carried))
             - self.coupling.at(low, high) * u
         )
-        near = self.sums(conc.at(low - rim, high + rim)) - 6.0 * c
+        near = self.sums(conc.at(low - 1, high + 1)) - 6.0 * c
         second = (
             right[1].at(low, high)
             - u
@@ -271,16 +276,32 @@
         )
         return first, second
 
-    def step(self, first, second, low):
-        high = low + first.shape[0]
+    def change(self, first, second, low, high):
         damp = self.damp.at(low, high)
         coupling = self.coupling.at(low, high)
-        conc_step = damp * (first - coupling * second)
-        return Strip(low, conc_step), Strip(low, damp * (second + self.diagonal * first))
+        return damp * (first - coupling * second), damp * (second + self.diagonal * first)
+
+    def residual(self, conc, chem, right, low, high):
+        if self.wrap:
+            conc, chem = wrapped(conc), wrapped(chem)
+        parts = self.pieces(lambda *at: self.defect(conc, chem, right, *at), low, high)
+        return tuple(part.cells for part in parts)
+
+    def step(self, right, low, high):
+        def work(low, high):
+            return self.change(right[0].at(low, high), right[1].at(low, high), low, high)
+
+        return self.pieces(work, low, high)
 
     def sweep(self, conc, chem, right, low, high):
-        dc, du = self.step(*self.residual(conc, chem, right, low, high), low)
-        return Strip(low, conc.at(low, high) + dc.cells), Strip(low, chem.at(low, high) + du.cells)
+        if self.wrap:
+            conc, chem = wrapped(conc), wrapped(chem)
+
+        def work(low, high):
+            dc, du = self.change(*self.defect(conc, chem, right, low, high), low, high)
+            return conc.at(low, high) + dc, chem.at(low, high) + du
+
+        return self.pieces(work, low, high)
 
     def sweeps(self, count, conc, chem, right):
         size = conc.cells.shape[0]
@@ -495,12 +516,10 @@
     mob2_waits = gather(1)
 
     arrive(beside)
-    level0 = Level(1.0, 1, 1)
+    level0 = Level(1.0, 1, 1, 2)
     middle = fields_of(0, (conc, chem), from_y0[0], from_y0[1])
     mob_middle = Strip(0, mobility_of(middle[0].cells))
-    coupling = Strip(1, level0.coupled(mob_middle.at(1, size - 1), level0.sums(mob_middle.cells)))
-    level0.set(mob_middle, coupling)
-    damp_middle = level0.damp
+    coupling, damp = level0.setup(mob_middle, 1, size - 1)
     right_middle = right_of_strip(middle[0])
     once_middle = level0.sweep(*middle, right_middle, 1, size - 1)
     both_middle = level0.sweep(*once_middle, right_middle, 2, size - 2)
@@ -527,16 +546,10 @@
     whole1[1] = jnp.where(even1, mob1, mob1_sum)
     mob1_waits, _ = swap1(1, HALO)
 
-    def outer_coupling(low, high):
-        near = level0.sums(mob0.at(low - 1, high + 1))
-        return Strip(low, level0.coupled(mob0.at(low, high), near))
-
-    coupling_low, coupling_high = outer_coupling(-3, 1), outer_coupling(size - 1, size + 3)
-    level0.set(mob0, coupling_low)
-    damp_low = level0.damp
-    level0.set(mob0, coupling_high)
-    level0.damp = strips(damp_low, damp_middle, level0.damp)
+    coupling_low, damp_low = level0.setup(mob0, -3, 1)
+    coupling_high, damp_high = level0.setup(mob0, size - 1, size + 3)
     level0.coupling = strips(coupling_low, coupling, coupling_high)
+    level0.damp = strips(damp_low, damp, damp_high)
 
     def completed(now, before, low, high):
         inner = now[0].start, now[0].start + now[0].cells.shape[0]
@@ -556,8 +569,8 @@
 
     arrive(mob1_waits)
     mob1, mob1_sum = spread(padded1(1, HALO), 1, 2)
-    level1 = Level(0.25, 1, 2)
-    level1.set(Strip(-HALO, mob1), Strip(-HALO, level1.coupled(mob1, mob1_sum)))
+    level1 = Level(0.25, 1, 2, 2)
+    level1.setup(Strip(-HALO, mob1), -HALO, half + HALO, Strip(-HALO, mob1_sum))
     drain(outer + beside + mob1_waits)
     def by_row(values):
         zero, one = spread(values, 1, 2)
@@ -569,15 +582,15 @@
     arrive(mob2_waits)
     mob2 = by_row(grid2[1, :, pl.ds(0, 4 * ny, stride=2)])
     mob3 = coarse(mob2, 4)
-    level2, level3 = Level(0.0625, 1, 4, True), Level(0.015625, 1, 8, True)
+    level2, level3 = Level(0.0625, 1, 4, 4, True), Level(0.015625, 1, 8, 4, True)
     for level, mob in ((level2, mob2), (level3, mob3)):
-        level.set(Strip(0, mob), Strip(0, level.coupled(mob, level.sums(mob))))
+        level.setup(wrapped(Strip(0, mob)), 0, mob.shape[0])
 
     drain(mob2_waits)
     arrive(near_waits)
     rhs1 = spread(padded1(0, 2), 1, 2)
-    conc, chem = level1.step(*rhs1, -2)
     rhs1 = [Strip(-2, values) for values in rhs1]
+    conc, chem = level1.step(rhs1, -2, half + 2)
     conc, chem = level1.sweep(conc, chem, rhs1, -1, half + 1)
     own = [
         twice_pair(pair_sum(pair_rows(values[:, :8]), 2, 2) * 0.125)
@@ -588,19 +601,19 @@
 
     arrive(far_waits)
     rhs1 = spread(padded1(0, HALO), 1, 2)
-    conc, chem = level1.step(*rhs1, -HALO)
     rhs1 = [Strip(-HALO, values) for values in rhs1]
+    conc, chem = level1.step(rhs1, -HALO, half + HALO)
     fields1 = level1.sweep(conc, chem, rhs1, -3, half + 3)
 
     drain(near_waits + far_waits)
     arrive(rhs2_waits)
     rhs2 = [by_row(grid2[0, :, pl.ds(start, 4 * ny, stride=2)]) for start in (0, 1)]
-    conc, chem = level2.step(*rhs2, 0)
     rhs2 = [Strip(0, values) for values in rhs2]
+    conc, chem = level2.step(rhs2, 0, nx * quarter)
     conc, chem = level2.sweep(conc, chem, rhs2, 0, nx * quarter)
     rhs3 = [coarse(v, 4) for v in level2.residual(conc, chem, rhs2, 0, nx * quarter)]
-    low_conc, low_chem = level3.step(*rhs3, 0)
     rhs3 = [Strip(0, values) for values in rhs3]
+    low_conc, low_chem = level3.step(rhs3, 0, nx * quarter // 2)
     low_conc, low_chem = level3.sweeps(COARSE - 1, low_conc, low_chem, rhs3)
     conc = Strip(0, conc.cells + twice(rows_twice(low_conc.cells)))
     chem = Strip(0, chem.cells + twice(rows_twice(low_chem.cells)))

time: 29.3 us -> 28.9 us (0.986)
  Pallas kernels: 26.8 us -> 26.4 us
    pallas_call x1, Pallas kernels: 26.8 us -> 26.4 us  [gathered_cycle(): pl.pallas_call(functools.partial(cycle_kernel, nx, ny), out_shape=shape,...]
where the time goes in v5:
time: 28.9 us; the launch traced here: 28.8 us
  Pallas kernels  26.4 us (91%)
  other arithmetic  0.99 us (3%)
  local copies, waits for them, and re-layouts  0.72 us (2%)
  between operations  0.64 us (2%)
    pallas_call x1, Pallas kernels, gathered_cycle(): pl.pallas_call(functools.partial(cycle_kernel, nx, ny), out_shape=shape,...  26.4 us
    another operation x1, other arithmetic, body(): result = gathered_cycle(nx, ny, jnp.stack([conc_old, chem_old]))  0.99 us
    squeeze x1, local copies, waits for them, and re-layouts, body(): return (result[0], result[1])  0.72 us

profile of v5, /device:TPU:0, one launch (start us, length us, event | category | flops | bytes accessed | tf_op | source)
XLA Modules:
  0.0 28.8 jit_solution(12390392638292971940)
XLA Ops:
  0.6 1.0 %pad_maximum_fusion.own = f32[2,16,16,128]{3,2,1,0:T(8,128)S(1)} fusion(f32[1,16,16,128]{3,2,1,0:T(8,128)} %bitcast.6, f32[1,16,16,128]{3,2,1,0:T(8,128)} %bitcast.7), kind=kLoop, calls=%fused_computation | loop fusion | flops 65536 | bytes 524288 | tf_op jit(solution)/shard_map/stack | solution.py:688
  1.6 26.4 %shard_map.41 = f32[2,16,16,128]{3,2,1,0:T(8,128)S(1)} custom-call(f32[2,16,16,128]{3,2,1,0:T(8,128)S(1)} %pad_maximum_fusion.own), custom_call_target="tpu_custom_call" | custom-call | tf_op jit(solution)/shard_map/pallas_call | solution.py:671
  28.0 0.7 %slice_bitcast_fusion = (f32[16,16,128]{2,1,0:T(8,128)}, f32[16,16,128]{2,1,0:T(8,128)}) fusion(f32[2,16,16,128]{3,2,1,0:T(8,128)S(1)} %shard_map.41), kind=kLoop, calls=%fused_computation.1 | loop fusion | bytes 524288 | tf_op jit(solution)/shard_map/squeeze | solution.py:691

commit v6 on v5

--- a/solution.py
+++ b/solution.py
@@ -511,10 +511,6 @@
         cells = conc.cells
         return conc, Strip(conc.start, cells * cells * cells - (1.0 + STABILIZER) * cells)
 
-    mob1 = coarse(mobility_of(conc), 1)
-    pack2[1] = by_lane(twice_pair(pair_sum(pair_rows(mob1), 2, 2) * 0.125))
-    mob2_waits = gather(1)
-
     arrive(beside)
     level0 = Level(1.0, 1, 1, 2)
     middle = fields_of(0, (conc, chem), from_y0[0], from_y0[1])
@@ -545,6 +541,7 @@
     even1 = iota((half, 8, 128), 2) % 2 == 0
     whole1[1] = jnp.where(even1, mob1, mob1_sum)
     mob1_waits, _ = swap1(1, HALO)
+    pack2[1] = by_lane(twice_pair(pair_sum(pair_rows(mob1), 2, 2) * 0.125))
 
     coupling_low, damp_low = level0.setup(mob0, -3, 1)
     coupling_high, damp_high = level0.setup(mob0, size - 1, size + 3)
@@ -566,27 +563,13 @@
     )
     whole1[0] = jnp.where(even1, coarse(first, 1), coarse(second, 1))
     near_waits, far_waits = swap1(0, 2)
+    mob2_waits = gather(1)
 
     arrive(mob1_waits)
     mob1, mob1_sum = spread(padded1(1, HALO), 1, 2)
     level1 = Level(0.25, 1, 2, 2)
     level1.setup(Strip(-HALO, mob1), -HALO, half + HALO, Strip(-HALO, mob1_sum))
     drain(outer + beside + mob1_waits)
-    def by_row(values):
-        zero, one = spread(values, 1, 2)
-        zero, two = spread(zero, 2, 2)
-        one, three = spread(one, 2, 2)
-        together = jnp.stack([zero, one, two, three], 1)
-        return together.reshape((nx * quarter,) + values.shape[1:])
-
-    arrive(mob2_waits)
-    mob2 = by_row(grid2[1, :, pl.ds(0, 4 * ny, stride=2)])
-    mob3 = coarse(mob2, 4)
-    level2, level3 = Level(0.0625, 1, 4, 4, True), Level(0.015625, 1, 8, 4, True)
-    for level, mob in ((level2, mob2), (level3, mob3)):
-        level.setup(wrapped(Strip(0, mob)), 0, mob.shape[0])
-
-    drain(mob2_waits)
     arrive(near_waits)
     rhs1 = spread(padded1(0, 2), 1, 2)
     rhs1 = [Strip(-2, values) for values in rhs1]
@@ -605,7 +588,21 @@
     conc, chem = level1.step(rhs1, -HALO, half + HALO)
     fields1 = level1.sweep(conc, chem, rhs1, -3, half + 3)
 
-    drain(near_waits + far_waits)
+    def by_row(values):
+        zero, one = spread(values, 1, 2)
+        zero, two = spread(zero, 2, 2)
+        one, three = spread(one, 2, 2)
+        together = jnp.stack([zero, one, two, three], 1)
+        return together.reshape((nx * quarter,) + values.shape[1:])
+
+    arrive(mob2_waits)
+    mob2 = by_row(grid2[1, :, pl.ds(0, 4 * ny, stride=2)])
+    mob3 = coarse(mob2, 4)
+    level2, level3 = Level(0.0625, 1, 4, 4, True), Level(0.015625, 1, 8, 4, True)
+    for level, mob in ((level2, mob2), (level3, mob3)):
+        level.setup(wrapped(Strip(0, mob)), 0, mob.shape[0])
+
+    drain(near_waits + far_waits + mob2_waits)
     arrive(rhs2_waits)
     rhs2 = [by_row(grid2[0, :, pl.ds(start, 4 * ny, stride=2)]) for start in (0, 1)]
     rhs2 = [Strip(0, values) for values in rhs2]

time: 28.9 us -> 28.1 us (0.972)
  Pallas kernels: 26.4 us -> 25.6 us
    pallas_call x1, Pallas kernels: 26.4 us -> 25.6 us  [gathered_cycle(): pl.pallas_call(functools.partial(cycle_kernel, nx, ny), out_shape=shape,...]
where the time goes in v6:
time: 28.1 us; the launch traced here: 27.9 us
  Pallas kernels  25.6 us (91%)
  other arithmetic  0.99 us (4%)
  local copies, waits for them, and re-layouts  0.72 us (3%)
  between operations  0.64 us (2%)
    pallas_call x1, Pallas kernels, gathered_cycle(): pl.pallas_call(functools.partial(cycle_kernel, nx, ny), out_shape=shape,...  25.6 us
    another operation x1, other arithmetic, body(): result = gathered_cycle(nx, ny, jnp.stack([conc_old, chem_old]))  0.99 us
    squeeze x1, local copies, waits for them, and re-layouts, body(): return (result[0], result[1])  0.72 us

profile of v6, /device:TPU:0, one launch (start us, length us, event | category | flops | bytes accessed | tf_op | source)
XLA Modules:
  0.0 27.9 jit_solution(10783531934682170754)
XLA Ops:
  0.6 1.0 %pad_maximum_fusion.own = f32[2,16,16,128]{3,2,1,0:T(8,128)S(1)} fusion(f32[1,16,16,128]{3,2,1,0:T(8,128)} %bitcast.6, f32[1,16,16,128]{3,2,1,0:T(8,128)} %bitcast.7), kind=kLoop, calls=%fused_computation | loop fusion | flops 65536 | bytes 524288 | tf_op jit(solution)/shard_map/stack | solution.py:685
  1.6 25.6 %shard_map.41 = f32[2,16,16,128]{3,2,1,0:T(8,128)S(1)} custom-call(f32[2,16,16,128]{3,2,1,0:T(8,128)S(1)} %pad_maximum_fusion.own), custom_call_target="tpu_custom_call" | custom-call | tf_op jit(solution)/shard_map/pallas_call | solution.py:668
  27.2 0.7 %slice_bitcast_fusion = (f32[16,16,128]{2,1,0:T(8,128)}, f32[16,16,128]{2,1,0:T(8,128)}) fusion(f32[2,16,16,128]{3,2,1,0:T(8,128)S(1)} %shard_map.41), kind=kLoop, calls=%fused_computation.1 | loop fusion | bytes 524288 | tf_op jit(solution)/shard_map/squeeze | solution.py:688
